TPU v7x, 32 devices: a whole 2x2x4 slice. The times are simulated.
32 devices in a mesh: dp: 2 (over x), heads: 4 (over y, core), tensor: 4 (over z).
Axes of the slice: x: 2, y: 2, z: 4, core: 2. Of those that a mesh axis runs over, the one named last changes fastest.
Arguments:
- patches: bfloat16 [64, 196, 768], P(('dp', 'tensor')), may hold values from -6 to 6
- masked: int32 [64, 75], P(('dp', 'tensor')), may hold values from 0 to 195, as said below
- targets: int32 [64, 75], P('dp'), may hold values from 0 to 8191
- patch_weight: float32 [768, 768], P(('dp', 'heads', 'tensor')), may hold values from -0.21875 to 0.21875
- patch_first: float32 [768, 768], P(('dp', 'heads', 'tensor')), may hold values from -0.003125 to 0.003125
- patch_second: float32 [768, 768], P(('dp', 'heads', 'tensor')), may hold values from 1.0850695e-06 to 4.340278e-06
- attention_weight: float32 [2, 768, 3072], P(None, ('dp', 'tensor'), 'heads')
- attention_first: float32 [2, 768, 3072], P(None, ('dp', 'tensor'), 'heads'), may hold values from -0.003125 to 0.003125
- attention_second: float32 [2, 768, 3072], P(None, ('dp', 'tensor'), 'heads'), may hold values from 1.0850695e-06 to 4.340278e-06
- hidden_weight: float32 [2, 2, 768, 3072], P(None, None, ('dp', 'heads'), 'tensor'), may hold values from -0.21875 to 0.21875
- hidden_first: float32 [2, 2, 768, 3072], P(None, None, ('dp', 'heads'), 'tensor'), may hold values from -0.003125 to 0.003125
- hidden_second: float32 [2, 2, 768, 3072], P(None, None, ('dp', 'heads'), 'tensor'), may hold values from 1.0850695e-06 to 4.340278e-06
- head_weight: float32 [768, 8192], P(('dp', 'heads'), 'tensor'), may hold values from -0.4375 to 0.4375
- head_first: float32 [768, 8192], P(('dp', 'heads'), 'tensor'), may hold values from -0.00047841595 to 0.00047841595
- head_second: float32 [768, 8192], P(('dp', 'heads'), 'tensor'), may hold values from 2.5431316e-08 to 1.0172526e-07
- vector_table: float32 [16, 768], replicated
- vector_first: float32 [16, 768], replicated, may hold values from -0.003125 to 0.003125
- vector_second: float32 [16, 768], replicated, may hold values from 1.0850695e-06 to 4.340278e-06
- relative_bias: float32 [12, 732], replicated, may hold values from -3 to 3
- bias_first: float32 [12, 732], replicated, may hold values from -0.00015625 to 0.00015625
- bias_second: float32 [12, 732], replicated, may hold values from 2.7126736e-09 to 1.0850695e-08
Outputs:
- loss: float32 [], replicated
- updated_patch: float32 [768, 768], P(('dp', 'heads', 'tensor'))
- moment_patch: float32 [768, 768], P(('dp', 'heads', 'tensor'))
- square_patch: float32 [768, 768], P(('dp', 'heads', 'tensor'))
- updated_attention: float32 [2, 768, 3072], P(None, ('dp', 'tensor'), 'heads')
- moment_attention: float32 [2, 768, 3072], P(None, ('dp', 'tensor'), 'heads')
- square_attention: float32 [2, 768, 3072], P(None, ('dp', 'tensor'), 'heads')
- updated_hidden: float32 [2, 2, 768, 3072], P(None, None, ('dp', 'heads'), 'tensor')
- moment_hidden: float32 [2, 2, 768, 3072], P(None, None, ('dp', 'heads'), 'tensor')
- square_hidden: float32 [2, 2, 768, 3072], P(None, None, ('dp', 'heads'), 'tensor')
- updated_head: float32 [768, 8192], P(('dp', 'heads'), 'tensor')
- moment_head: float32 [768, 8192], P(('dp', 'heads'), 'tensor')
- square_head: float32 [768, 8192], P(('dp', 'heads'), 'tensor')
- updated_vectors: float32 [16, 768], replicated
- moment_vectors: float32 [16, 768], replicated
- square_vectors: float32 [16, 768], replicated
- updated_bias: float32 [12, 732], replicated
- moment_bias: float32 [12, 732], replicated
- square_bias: float32 [12, 732], replicated
Inputs may be any that keep to these rules, and one draw needn't show every extreme that they name: `masked`: the 75 entries of an image are different patch numbers.
All inputs are finite; a program needn't handle non-finite values.
Results may differ from a plain program's by a relative error of at most 0.015.
The roundings to bfloat16 on the way count: a program that leaves them out, or rounds other values in their place, can miss the bound.
Values may be sent and summed in bfloat16 or wider, within the bound.
No kernel may reach another device: no remote copies, remote signals or barrier semaphores. Data moves between devices by JAX's collectives and lax.ppermute only.
A program may use at most 256 MiB of HBM per device.

v0:
```python
from functools import partial

import jax
import jax.numpy as jnp
import numpy as np
from jax import lax
from jax.experimental import pallas as pl
from jax.experimental.pallas import tpu as pltpu
from jax.sharding import PartitionSpec as P

HEAD_DIM = 64
GRID = 14
STEP = 3
CORES = 2

epsilon = 1e-06
beta_one = 0.5
beta_two = 0.5
adam_floor = 1e-08
decay_rate = 0.05
learning_rates = (0.03, 0.03, 0.02, 0.03, 0.3, 0.3)
highest = lax.Precision.HIGHEST
ANY = pl.BlockSpec(memory_space=pl.ANY)
LIGHT = pl.CostEstimate(flops=1, bytes_accessed=1, transcendentals=0)
SMEM = pl.BlockSpec(memory_space=pltpu.SMEM)


class Place:
    def __init__(self):
        heads = lax.axis_size("heads")
        self.short = (lax.axis_size("dp"), heads, lax.axis_size("tensor")) == (2, 4, 4)
        self.size = {
            "x": lax.axis_size("dp"),
            "y": heads // CORES,
            "c": CORES,
            "z": lax.axis_size("tensor"),
        }
        head_at = lax.axis_index("heads")
        self.at = {
            "x": lax.axis_index("dp"),
            "y": head_at // CORES,
            "c": head_at % CORES,
            "z": lax.axis_index("tensor"),
        }
        self.scalars = jnp.stack([self.at[k] for k in "xycz"]).astype(jnp.int32)

    def hop(self, value, way):
        count = self.size[way]
        if way in "xz":
            axis = "dp" if way == "x" else "tensor"
            return lax.ppermute(value, axis, [(i, (i + 1) % count) for i in range(count)])
        if way == "y":
            pairs = [
                (i * CORES + c, (i + 1) % count * CORES + c)
                for i in range(count)
                for c in range(CORES)
            ]
        else:
            pairs = [
                (i * CORES + c, i * CORES + (c + 1) % CORES)
                for i in range(self.size["y"])
                for c in range(CORES)
            ]
        return lax.ppermute(value, "heads", pairs)

    def ring(self, value, way):
        held = [value]
        for _ in range(self.size[way] - 1):
            held.append(self.hop(held[-1], way))
        return held


def owner(scalars, sizes, ways, steps):
    index = 0
    for way in ways:
        mine = scalars["xycz".index(way)]
        behind = lax.rem(mine + sizes[way] - steps[way], sizes[way])
        index = index * sizes[way] + behind
    return index


def ordered(place, value, dim, way):
    count = place.size[way]
    turned = jnp.flip(value, dim)
    return lax.dynamic_slice_in_dim(
        jnp.concatenate([turned, turned], dim), count - 1 - place.at[way], count, dim
    )


class Gather:
    def __init__(self, place, shard):
        self.place = place
        self.ring, self.held, self.flying = [shard], {}, {}

    def start(self, kind):
        place, held, out = self.place, self.held, []
        if kind == "z":
            out.append((None, place.hop(self.ring[-1], "z")))
        elif kind == "one":
            self.own = jnp.stack(self.ring)
            held[0, 0, 0, 0] = self.own
            out.append(((0, 1, 0, 0), place.hop(self.own, "y")))
            out.append(((1, 0, 0, 0), place.hop(self.own, "x")))
        elif kind == "two":
            axis = 0 if len(self.ring) > 1 else 2
            half = self.own.shape[axis] // 2
            low = lax.slice_in_dim(held[0, 1, 0, 0], 0, half, axis=axis)
            high = lax.slice_in_dim(held[1, 0, 0, 0], half, 2 * half, axis=axis)
            out.append(((1, 1, 0, 0), place.hop(low, "x")))
            out.append(((1, 1, 0, half if axis == 0 else 1), place.hop(high, "y")))
        else:
            for key in [k for k in sorted(held) if k[2] == 0]:
                other = (key[0], key[1], 1, key[3])
                if other not in held:
                    held[other] = None
                    out.append((other, place.hop(held[key], "c")))
        self.flying[kind] = out

    def load(self, kind):
        return [value for _, value in self.flying[kind]]

    def land(self, kind, values):
        for (key, _), value in zip(self.flying.pop(kind), values, strict=True):
            if key is None:
                self.ring.append(value)
            else:
                self.held[key] = value


def merged(kept, arrived, keys, halves, whole, out_type):
    count, depth = len(kept), kept[0].shape[2]
    r, c = kept[0].shape[3:]
    half = depth // 2
    split = out_type == "split"
    kind = jnp.float32 if out_type == "own" else jnp.bfloat16
    blocks, operands, kinds = [], [], []
    for key in keys:
        for m in range(count):
            for source in (kept[m], arrived[m]):
                blocks.append(pl.BlockSpec((1, 1, 1, r, c), lambda i, k=key: (*k, i, 0, 0)))
                operands.append(source)
    low_map = lambda i: (0, jnp.minimum(i, half - 1), 0, 0)
    high_map = lambda i: (0, jnp.maximum(i - half, 0), 0, 0)
    for side in halves:
        blocks.append(pl.BlockSpec((count, 1, r, c), high_map if side[0] else low_map))
        operands.append(side[1])
    for value in whole:
        blocks.append(pl.BlockSpec((count, 1, r, c), lambda i: (0, i, 0, 0)))
        operands.append(value)
    if split:
        shapes = [jax.ShapeDtypeStruct((count, half, r, c), kind)] * 2
        specs = [pl.BlockSpec((count, 1, r, c), m) for m in (low_map, high_map)]
    else:
        shapes = [jax.ShapeDtypeStruct((count, depth, r, c), kind)] * len(keys)
        specs = [pl.BlockSpec((count, 1, r, c), lambda i: (0, i, 0, 0))] * len(keys)

    def body(*refs):
        ins, outs = refs[: len(operands)], refs[len(operands) :]
        step = pl.program_id(0)
        base = 2 * count * len(keys)
        for n in range(len(keys)):
            for m in range(count):
                at = 2 * (n * count + m)
                total = ins[at][0, 0, 0] + ins[at + 1][0, 0, 0].astype(jnp.float32)
                for extra in ins[base + len(halves) :]:
                    total = total + extra[m, 0].astype(jnp.float32)
                if split:
                    for upper, out in enumerate(outs):

                        @pl.when((step >= half) if upper else (step < half))
                        def _(out=out, total=total):
                            out[m, 0] = total.astype(kind)
                elif halves:
                    upper = halves[n][0]
                    more = ins[base + n][m, 0].astype(jnp.float32)
                    here = (step >= half) if upper else (step < half)
                    outs[n][m, 0] = (total + jnp.where(here, more, 0.0)).astype(kind)
                else:
                    outs[n][m, 0] = total.astype(kind)

    return pl.pallas_call(
        body,
        out_shape=shapes,
        grid=(depth,),
        in_specs=blocks,
        out_specs=specs,
        compiler_params=pltpu.CompilerParams(vmem_limit_bytes=32 * 2**20),
        cost_estimate=LIGHT,
    )(*operands)


class Scatter:
    def __init__(self, place, sent, kept):
        self.place, self.state, self.total = place, "c", None
        self.flying = [place.hop(s, "c") for s in sent]
        self.kept, self.depth = kept, kept[0].shape[2]

    def view(self, values):
        if self.depth > 1:
            return values
        return [v.reshape(v.shape[:2] + (2, v.shape[3] // 2, v.shape[4])) for v in values]

    def land(self, values):
        place, self.flying = self.place, []
        if self.state == "c":
            self.kept, self.near = self.view(self.kept), self.view(values)
            low, high = merged(self.kept, self.near, [(1, 1)], [], [], "split")
            self.flying = [place.hop(low, "y"), place.hop(high, "x")]
            self.state = "two"
        elif self.state == "two":
            x, y = merged(
                self.kept, self.near, [(1, 0), (0, 1)], [(0, values[0]), (1, values[1])], [], "low"
            )
            self.flying = [place.hop(x, "x"), place.hop(y, "y")]
            self.state = "one"
        elif self.state == "one":
            (self.own,) = merged(self.kept, self.near, [(0, 0)], [], list(values), "own")
            if self.depth == 1:
                shape = self.own.shape
                self.total = self.own.reshape(shape[0], 2 * shape[2], shape[3])
                self.state = "done"
            else:
                self.flying = [place.hop(self.own[:, 1].astype(jnp.bfloat16), "z")]
                self.step, self.state = 2, "z"
        else:
            running = values[0].astype(jnp.float32) + self.own[:, self.step % self.depth]
            if self.step % self.depth:
                self.flying = [place.hop(running.astype(jnp.bfloat16), "z")]
                self.step += 1
            else:
                self.total, self.state = running, "done"


class SmallSum:
    def __init__(self, place, value):
        self.place, self.ways, self.total = place, list("cxyz"), None
        self.send(value)

    def send(self, value):
        self.own, self.state = value, self.ways.pop(0)
        count = self.place.size[self.state]
        if self.state == "z":
            self.flying = [
                lax.ppermute(value, "tensor", [(i, (i + k) % count) for i in range(count)])
                for k in range(1, count)
            ]
        else:
            self.flying = [self.place.hop(value, self.state)]

    def land(self, values):
        self.flying, held = [], jnp.stack([self.own, *values])
        if len(values) > 1:
            held = ordered(self.place, held, 0, self.state)
        total = held[0]
        for entry in range(1, held.shape[0]):
            total = total + held[entry]
        if self.ways:
            self.send(total)
        else:
            self.total = total


def await_hops(waited, *values):
    loads = [group.load(kind) for group, kind in waited]
    out = lax.optimization_barrier(tuple(values) + tuple(v for load in loads for v in load))
    at = len(values)
    for (group, kind), load in zip(waited, loads, strict=True):
        group.land(kind, out[at : at + len(load)])
        at += len(load)
    return out[0] if len(values) == 1 else out[: len(values)]


def pump(movers, *values):
    active = [m for m in movers if m.flying]
    loads = [m.flying for m in active]
    out = lax.optimization_barrier(tuple(values) + tuple(v for load in loads for v in load))
    at = len(values)
    for mover, load in zip(active, loads, strict=True):
        mover.land(out[at : at + len(load)])
        at += len(load)
    return out[0] if len(values) == 1 else out[: len(values)]


def assemble(place, group, matrix, rows, row_ways, column_ways, base=0):
    sizes = place.size
    keys = sorted(group.held)
    some = group.held[0, 0, 0, 0]
    c = some.shape[-1]
    row_count = int(np.prod([sizes[w] for w in row_ways]))
    column_count = int(np.prod([sizes[w] for w in column_ways])) if column_ways else 1
    moves = []
    for n, (kx, ky, kc, more) in enumerate(keys):
        held = group.held[kx, ky, kc, more]
        shift = 0 if some.shape[0] > 1 else more * (rows // 2)
        height = min(rows, held.shape[2] - base)
        for kz in range(held.shape[0]):
            behind = dict(x=kx, y=ky, c=kc, z=kz + (more if some.shape[0] > 1 else 0))
            moves.append((n, kz, behind, shift, height))

    def body(scalars, *refs):
        ins, out, sems = refs[: len(keys)], refs[len(keys)], refs[len(keys) + 1]
        copies = []
        for at, (n, kz, behind, shift, height) in enumerate(moves):
            row = owner(scalars, sizes, row_ways, behind) * rows + shift
            row = pl.multiple_of(row, int(np.gcd(rows, shift) if shift else rows))
            column = pl.multiple_of(owner(scalars, sizes, column_ways, behind) * c, c)
            copies.append(
                pltpu.make_async_copy(
                    ins[n].at[kz, matrix, pl.ds(base, height)],
                    out.at[pl.ds(row, height), pl.ds(column, c)],
                    sems.at[at],
                )
            )
        for copy in copies:
            copy.start()
        for copy in copies:
            copy.wait()

    return pl.pallas_call(
        body,
        out_shape=jax.ShapeDtypeStruct((row_count * rows, column_count * c), some.dtype),
        in_specs=[SMEM] + [ANY] * len(keys),
        out_specs=pl.BlockSpec(memory_space=pltpu.VMEM),
        scratch_shapes=[pltpu.SemaphoreType.DMA((len(moves),))],
        compiler_params=pltpu.CompilerParams(vmem_limit_bytes=24 * 2**20),
        cost_estimate=LIGHT,
    )(place.scalars, *[group.held[k] for k in keys])


def contract_first(left_side, right_side):
    return lax.dot_general(
        left_side, right_side, (((0,), (0,)), ((), ())), preferred_element_type=jnp.float32
    )


def packed_gradient(place, pairs, row_ways, column_ways):
    sizes = place.size
    tokens, wide = pairs[0][0].shape
    column_count = int(np.prod([sizes[w] for w in column_ways])) if column_ways else 1
    c = pairs[0][1].shape[1] // column_count
    r = wide // int(np.prod([sizes[w] for w in row_ways]))
    depth = sizes["z"] if "z" in row_ways + column_ways else 1
    by_core, by_rows = "c" in column_ways, "z" in row_ways
    steps = []
    if by_core:
        for kc in (1, 0):
            steps += [dict(c=kc, y=ky) for ky in range(sizes["y"])]
    elif column_ways:
        steps = [dict(z=kz) for kz in range(depth)]
    else:
        steps = [dict()]

    def column_of(i, scalars):
        if by_core:
            behind = dict(c=1 - i // sizes["y"], y=lax.rem(i, sizes["y"]))
        elif column_ways:
            behind = dict(z=i)
        else:
            return 0
        return owner(scalars, sizes, column_ways, behind)

    def body(scalars, *refs):
        ins = refs[: 2 * len(pairs)]
        sent, kept, work = refs[2 * len(pairs) : 2 * len(pairs) + 3]
        turned = refs[2 * len(pairs) + 3 :]
        step = pl.program_id(0)

        @pl.when(step == 0)
        def _():
            for left, across in zip(ins[::2], turned, strict=True):
                across[...] = left[...].T

        total = None
        for across, right in zip(turned, ins[1::2], strict=True):
            part = jnp.dot(across[...], right[...], preferred_element_type=jnp.float32)
            total = part if total is None else total + part
        work[...] = total
        blocks = [
            dict(zip(row_ways, ks))
            for ks in np.ndindex(*[sizes[w] for w in row_ways])
        ]

        def place_blocks(out, kc):
            for ks in blocks:
                if "c" in ks and ks["c"] != kc:
                    continue
                start = pl.multiple_of(owner(scalars, sizes, row_ways, ks) * r, r)
                block = work[pl.ds(start, r), :].astype(out.dtype)
                at = (ks["x"], 0 if by_core else ks["y"], ks.get("z", 0))
                out[at] = block

        if by_core:
            pl.when(step < sizes["y"])(lambda: place_blocks(sent, 1))
            pl.when(step >= sizes["y"])(lambda: place_blocks(kept, 0))
        else:
            place_blocks(sent, 1)
            place_blocks(kept, 0)

    if by_core:
        block = (sizes["x"], 1, depth, r, c)
        last = sizes["y"] - 1
        sent_map = lambda i, s: (0, jnp.minimum(i, last), 0, 0, 0)
        kept_map = lambda i, s: (0, jnp.maximum(i - last - 1, 0), 0, 0, 0)
    else:
        block = (sizes["x"], sizes["y"], depth if by_rows else 1, r, c)
        sent_map = kept_map = lambda i, s: (0, 0, i, 0, 0)
    shape = (sizes["x"], sizes["y"], depth, r, c)
    in_specs, operands = [], []
    for left, right in pairs:
        in_specs += [
            pl.BlockSpec((tokens, wide), lambda i, s: (0, 0)),
            pl.BlockSpec((tokens, c), lambda i, s: (0, column_of(i, s))),
        ]
        operands += [left, right]
    return pl.pallas_call(
        body,
        out_shape=(
            jax.ShapeDtypeStruct(shape, jnp.bfloat16),
            jax.ShapeDtypeStruct(shape, jnp.float32),
        ),
        grid_spec=pltpu.PrefetchScalarGridSpec(
            num_scalar_prefetch=1,
            grid=(len(steps),),
            in_specs=in_specs,
            out_specs=(pl.BlockSpec(block, sent_map), pl.BlockSpec(block, kept_map)),
            scratch_shapes=[pltpu.VMEM((wide, c), jnp.float32)]
            + [pltpu.VMEM((wide, tokens), jnp.bfloat16) for _ in pairs],
        ),
        compiler_params=pltpu.CompilerParams(vmem_limit_bytes=48 * 2**20),
        cost_estimate=LIGHT,
    )(place.scalars, *operands)


AXES = {"x": ("dp",), "yc": ("heads",), "z": ("tensor",)}


def axes_of(ways):
    names = []
    for part in ("x", "yc", "z"):
        if part in ways:
            names.append((ways.index(part), AXES[part][0]))
    return tuple(name for _, name in sorted(names))


def scatter_sum(value, ways):
    shape = value.shape[len(ways) :]
    for part in ("x", "yc", "z"):
        at = ways.find(part)
        if at >= 0:
            merged = value.shape[:at] + (-1,) + value.shape[at + len(part) :]
            value = lax.psum_scatter(value.reshape(merged), AXES[part][0], scatter_dimension=at)
            ways = ways[:at] + ways[at + len(part) :]
    return value.reshape(shape)


def relative_tables(grid_side, padded):
    reach = 2 * grid_side - 1
    rows = np.arange(grid_side)
    delta = rows[:, None] - rows[None, :] + grid_side - 1
    one = (delta[:, :, None] == np.arange(reach)[None, None, :]).astype(np.float32)
    spread = np.einsum("rs,cmb->crbsm", np.eye(grid_side, dtype=np.float32), one)
    spread = spread.reshape(grid_side, grid_side * reach, grid_side * grid_side)
    down = -spread.shape[1] % 128
    across = padded + -padded % 128 - grid_side * grid_side
    spread = np.pad(spread, ((0, 0), (0, down), (0, across)))
    return one, jnp.asarray(spread, jnp.bfloat16)


def thirds(value):
    terms = []
    for _ in range(3):
        terms.append(value.astype(jnp.bfloat16))
        value = value - terms[-1].astype(jnp.float32)
    return jnp.concatenate(terms, 0)


def sum_thirds(value):
    third = value.shape[0] // 3
    return value[:third] + value[third : 2 * third] + value[2 * third :]


def bias_expand(table, grid_side, padded):
    one, spread = relative_tables(grid_side, padded)
    heads = table.shape[0]
    reach, side = 2 * grid_side - 1, grid_side * grid_side
    tall = -(-grid_side // 16) * 16
    inner = table[:, : reach * reach].reshape(heads, reach, reach)
    rows = jnp.einsum("hab,rsa->hrsb", inner, one, precision=highest)
    rows = rows.reshape(heads, grid_side, grid_side * reach)
    rows = jnp.pad(
        rows, ((0, 0), (0, tall - grid_side), (0, spread.shape[1] - grid_side * reach))
    ).reshape(heads * tall, -1)

    lanes = spread.shape[2] // 128
    first = side // 16 * 16

    def body(rows_ref, corner_ref, spread_ref, out_ref, *works):
        column = lax.broadcasted_iota(jnp.int32, (tall, lanes * 128), 1)
        line = lax.broadcasted_iota(jnp.int32, (padded - first, lanes * 128), 0) + first
        across = lax.broadcasted_iota(jnp.int32, line.shape, 1)
        for h in range(heads):
            last = jnp.where(across < side, corner_ref[h, 0], corner_ref[h, 2])
            last = jnp.where(line == side, last, 0.0)
            last = jnp.where(across > side, -1e30, last)
            for i, work in enumerate(works):
                work[h, first:, :] = last[:, 128 * i : 128 * (i + 1)]
        terms = thirds(rows_ref[...])
        for c in range(grid_side):
            full = sum_thirds(
                jnp.dot(terms, spread_ref[c], preferred_element_type=jnp.float32)
            )
            for h in range(heads):
                block = full[h * tall : (h + 1) * tall]
                block = jnp.where(column == side, corner_ref[h, 1], block)
                block = jnp.where(column > side, -1e30, block)[:grid_side]
                for i, work in enumerate(works):
                    work[h, pl.ds(c, grid_side, stride=grid_side), :] = block[
                        :, 128 * i : 128 * (i + 1)
                    ]
        for h in range(heads):
            whole = jnp.concatenate([work[h] for work in works], 1)
            out_ref[h] = whole[:, :padded]

    vmem = pl.BlockSpec(memory_space=pltpu.VMEM)
    return pl.pallas_call(
        body,
        out_shape=jax.ShapeDtypeStruct((heads, padded, padded), jnp.float32),
        in_specs=[vmem, SMEM, vmem],
        out_specs=vmem,
        scratch_shapes=[pltpu.VMEM((heads, padded, 128), jnp.float32)] * lanes,
        compiler_params=pltpu.CompilerParams(vmem_limit_bytes=32 * 2**20),
        cost_estimate=LIGHT,
    )(rows, table[:, reach * reach :], spread)


def bias_corners(grad, grid_side):
    side = grid_side * grid_side
    return jnp.stack(
        [
            jnp.sum(grad[:, side, :side], -1),
            jnp.sum(grad[:, :side, side], -1),
            grad[:, side, side],
        ],
        1,
    )


def bias_rows(grad, grid_side):
    heads, padded = grad.shape[:2]
    _, spread = relative_tables(grid_side, padded)
    tall = -(-grid_side // 16) * 16

    lanes = spread.shape[2] // 128

    def body(grad_ref, spread_ref, out_ref, work, *wholes):
        work[...] = jnp.zeros_like(work)
        for h in range(heads):
            for i, whole in enumerate(wholes):
                until = min(padded, 128 * (i + 1))
                if until < 128 * (i + 1):
                    whole[h] = jnp.zeros((padded, 128), jnp.float32)
                whole[h, :, : until - 128 * i] = grad_ref[h, :, 128 * i : until]
        total = None
        for c in range(grid_side):
            for h in range(heads):
                for i, whole in enumerate(wholes):
                    work[h * tall : h * tall + grid_side, 128 * i : 128 * (i + 1)] = whole[
                        h, pl.ds(c, grid_side, stride=grid_side), :
                    ]
            part = sum_thirds(contract_columns(thirds(work[...]), spread_ref[c]))
            total = part if total is None else total + part
        out_ref[...] = total

    vmem = pl.BlockSpec(memory_space=pltpu.VMEM)
    return pl.pallas_call(
        body,
        out_shape=jax.ShapeDtypeStruct((heads * tall, spread.shape[1]), jnp.float32),
        in_specs=[vmem, vmem],
        out_specs=vmem,
        scratch_shapes=[pltpu.VMEM((heads * tall, 128 * lanes), jnp.float32)]
        + [pltpu.VMEM((heads, padded, 128), jnp.float32)] * lanes,
        compiler_params=pltpu.CompilerParams(vmem_limit_bytes=32 * 2**20),
        cost_estimate=LIGHT,
    )(grad, spread)


def bias_collect(rows, corners, grid_side):
    one, _ = relative_tables(grid_side, grid_side * grid_side)
    heads, reach = corners.shape[0], 2 * grid_side - 1
    rows = rows.reshape(heads, -1, rows.shape[1])[:, :grid_side, : grid_side * reach]
    rows = rows.reshape(heads, grid_side, grid_side, reach)
    inner = jnp.einsum("hrsb,rsa->hab", rows, one, precision=highest)
    return jnp.concatenate([inner.reshape(heads, -1), corners], 1)


def norm_parts(values):
    centred = values - jnp.mean(values, -1, keepdims=True)
    scaled = lax.rsqrt(jnp.mean(centred * centred, -1, keepdims=True) + epsilon)
    return centred * scaled, scaled


def norm_forward(values, added, table, gain_at, scale_at, parts):
    rows, wide = values.shape

    def body(*refs):
        table_ref, values_ref = refs[:2]
        outs = refs[len(operands) :]
        total = values_ref[...]
        if added is not None:
            total = total + table_ref[scale_at : scale_at + 1, :] * refs[2][...]
            outs[1][...] = total
        gain, shift = table_ref[gain_at : gain_at + 1, :], table_ref[gain_at + 1 : gain_at + 2, :]
        outs[0][...] = (norm_parts(total)[0] * gain + shift).astype(jnp.bfloat16)

    operands = [table, values] + ([] if added is None else [added])
    spec = pl.BlockSpec((rows // parts, wide), lambda i: (i, 0))
    shapes = [jax.ShapeDtypeStruct((rows, wide), jnp.bfloat16)]
    if added is not None:
        shapes.append(jax.ShapeDtypeStruct((rows, wide), jnp.float32))
    out = pl.pallas_call(
        body,
        out_shape=shapes,
        grid=(parts,),
        in_specs=[pl.BlockSpec(table.shape, lambda i: (0, 0))] + [spec] * (len(operands) - 1),
        out_specs=[spec] * len(shapes),
        compiler_params=pltpu.CompilerParams(vmem_limit_bytes=24 * 2**20),
        cost_estimate=LIGHT,
    )(*operands)
    return (out[0], values) if added is None else (out[0], out[1])


def norm_backward(values, grad, more, below, table, gain_at, scale_at, parts):
    rows, wide = values.shape

    def body(*refs):
        table_ref, values_ref, grad_ref = refs[:3]
        rest = list(refs[3 : len(operands)])
        outs = refs[len(operands) :]
        normed, scaled = norm_parts(values_ref[...])
        grads = grad_ref[...]
        inner = grads * table_ref[gain_at : gain_at + 1, :]
        total = scaled * (
            inner
            - jnp.mean(inner, -1, keepdims=True)
            - normed * jnp.mean(inner * normed, -1, keepdims=True)
        )
        if more is not None:
            total = total + rest.pop(0)[...]
        outs[0][...] = total
        sums = [jnp.sum(grads * normed, 0, keepdims=True), jnp.sum(grads, 0, keepdims=True)]
        if below is not None:
            sums.append(jnp.sum(total * rest.pop(0)[...], 0, keepdims=True))
            outs[2][...] = (total * table_ref[scale_at : scale_at + 1, :]).astype(jnp.bfloat16)
        sums.append(jnp.zeros((8 - len(sums), wide), jnp.float32))
        sums = jnp.concatenate(sums, 0)

        @pl.when(pl.program_id(0) == 0)
        def _():
            outs[1][...] = sums

        @pl.when(pl.program_id(0) > 0)
        def _():
            outs[1][...] += sums

    operands = [table, values, grad] + [v for v in (more, below) if v is not None]
    spec = pl.BlockSpec((rows // parts, wide), lambda i: (i, 0))
    shapes = [
        jax.ShapeDtypeStruct((rows, wide), jnp.float32),
        jax.ShapeDtypeStruct((8, wide), jnp.float32),
    ]
    specs = [spec, pl.BlockSpec((8, wide), lambda i: (0, 0))]
    if below is not None:
        shapes.append(jax.ShapeDtypeStruct((rows, wide), jnp.bfloat16))
        specs.append(spec)
    return pl.pallas_call(
        body,
        out_shape=shapes,
        grid=(parts,),
        in_specs=[pl.BlockSpec(table.shape, lambda i: (0, 0))] + [spec] * (len(operands) - 1),
        out_specs=specs,
        compiler_params=pltpu.CompilerParams(vmem_limit_bytes=32 * 2**20),
        cost_estimate=LIGHT,
    )(*operands)


def contract_rows(left_side, right_side):
    return lax.dot_general(
        left_side, right_side, (((0,), (0,)), ((), ())), preferred_element_type=jnp.float32
    )


def contract_columns(left_side, right_side):
    return lax.dot_general(
        left_side, right_side, (((1,), (1,)), ((), ())), preferred_element_type=jnp.float32
    )


def heads_of(block, width):
    scale = width ** (-0.5)
    for at in range(0, 3 * block.shape[1] // 4, 3 * width):
        query = block[:, at : at + width].astype(jnp.float32) * scale
        yield (
            query.astype(jnp.bfloat16),
            block[:, at + width : at + 2 * width],
            block[:, at + 2 * width : at + 3 * width],
        )


def softmax_of(query, key, bias):
    scores = contract_columns(query, key) + bias
    raised = jnp.exp(scores - jnp.max(scores, -1, keepdims=True))
    return raised / jnp.sum(raised, -1, keepdims=True)


def attention_forward(projected, bias_grid, images, groups, width):
    rows, total = projected.shape
    tokens, wide = rows // images, total // groups
    per_group = bias_grid.shape[0] // groups

    def body(block_ref, bias_ref, out_ref):
        out = []
        for j, (query, key, value) in enumerate(heads_of(block_ref[...], width)):
            weights = softmax_of(query, key, bias_ref[j]).astype(jnp.bfloat16)
            out.append(jnp.dot(weights, value, preferred_element_type=jnp.float32))
        out_ref[:, : wide * 3 // 4] = jnp.zeros((tokens, wide * 3 // 4), jnp.bfloat16)
        out_ref[:, wide * 3 // 4 :] = jnp.concatenate(out, 1).astype(jnp.bfloat16)

    spec = pl.BlockSpec((tokens, wide), lambda b, g: (g, b))
    return pl.pallas_call(
        body,
        out_shape=jax.ShapeDtypeStruct((rows, total), jnp.bfloat16),
        grid=(groups, images),
        in_specs=[spec, pl.BlockSpec((per_group, tokens, tokens), lambda b, g: (b, 0, 0))],
        out_specs=spec,
        compiler_params=pltpu.CompilerParams(vmem_limit_bytes=32 * 2**20),
        cost_estimate=LIGHT,
    )(projected, bias_grid)


def attention_backward(projected, grad_context, bias_grid, bias_grad, images, groups, width):
    rows, total = projected.shape
    tokens, wide = rows // images, total // groups
    per_group = bias_grid.shape[0] // groups

    def body(block_ref, grad_ref, bias_ref, before_ref, out_ref, bias_out):
        image = pl.program_id(1)

        @pl.when(image == 0)
        def _():
            bias_out[...] = before_ref[...]

        out = []
        grads = grad_ref[:, wide * 3 // 4 :]
        for j, (query, key, value) in enumerate(heads_of(block_ref[...], width)):
            weights = softmax_of(query, key, bias_ref[j])
            grad = grads[:, j * width : (j + 1) * width]
            grad_weights = contract_columns(grad, value)
            grad_value = contract_first(weights.astype(jnp.bfloat16), grad)
            inner = jnp.sum(weights * grad_weights, -1, keepdims=True)
            grad_scores = weights * (grad_weights - inner)
            bias_out[j] += grad_scores
            rounded = grad_scores.astype(jnp.bfloat16)
            grad_query = jnp.dot(rounded, key, preferred_element_type=jnp.float32) * width ** (-0.5)
            out += [grad_query, contract_first(rounded, query), grad_value]
        out_ref[:, : wide * 3 // 4] = jnp.concatenate(out, 1).astype(jnp.bfloat16)
        out_ref[:, wide * 3 // 4 :] = jnp.zeros((tokens, wide // 4), jnp.bfloat16)

    spec = pl.BlockSpec((tokens, wide), lambda b, g: (g, b))
    bias_spec = pl.BlockSpec((per_group, tokens, tokens), lambda b, g: (b, 0, 0))
    return pl.pallas_call(
        body,
        out_shape=(
            jax.ShapeDtypeStruct((rows, total), jnp.bfloat16),
            jax.ShapeDtypeStruct(bias_grid.shape, jnp.float32),
        ),
        grid=(groups, images),
        in_specs=[spec, spec, bias_spec, bias_spec],
        out_specs=(spec, bias_spec),
        compiler_params=pltpu.CompilerParams(vmem_limit_bytes=40 * 2**20),
        cost_estimate=LIGHT,
    )(projected, grad_context, bias_grid, bias_grad)


def gelu_parts(hidden):
    below = 0.5 * (1.0 + lax.erf(hidden * np.float32(0.5**0.5)))
    density = jnp.exp(-0.5 * hidden * hidden) * np.float32((2.0 * np.pi) ** -0.5)
    return hidden * below, below + hidden * density


def adam_update(weight, first_moment, second_moment, gradient, rate):
    first_new = beta_one * first_moment + (1.0 - beta_one) * gradient
    second_new = beta_two * second_moment + (1.0 - beta_two) * gradient * gradient
    first_fix = 1.0 - beta_one**STEP
    second_fix = 1.0 - beta_two**STEP
    stepped = first_new / first_fix / (jnp.sqrt(second_new / second_fix) + adam_floor)
    return (weight - rate * (stepped + decay_rate * weight), first_new, second_new)


def shards(
    patches,
    masked,
    targets,
    patch_weight,
    patch_first,
    patch_second,
    attention_weight,
    attention_first,
    attention_second,
    hidden_weight,
    hidden_first,
    hidden_second,
    head_weight,
    head_first,
    head_second,
    vector_table,
    vector_first,
    vector_second,
    relative_bias,
    bias_first,
    bias_second,
):
    place = Place()
    sizes = place.size
    heads_index = lax.axis_index("heads")
    heads_size = lax.axis_size("heads")
    tensor_index = lax.axis_index("tensor")
    tensor_size = lax.axis_size("tensor")
    images = patches.shape[0] // heads_size
    patch_count = patches.shape[1]
    tokens = patch_count + 1
    marked = masked.shape[1]
    layer_count = attention_weight.shape[0]
    head_width = HEAD_DIM
    wide = patch_weight.shape[1]
    total_rows = patches.shape[0] * marked * lax.axis_size("dp") * tensor_size
    final_base = 6 * layer_count

    low = lambda a: a.astype(jnp.bfloat16)
    padded = -(-tokens // 16) * 16
    rows = images * padded

    own = lambda a: lax.dynamic_slice_in_dim(a, heads_index * images, images)
    own_masked = own(masked)
    token_ids = jnp.arange(padded)
    is_masked = jnp.any(own_masked[:, :, None] == token_ids[None, None, :], axis=1)[:, :, None]
    is_class = (token_ids == patch_count)[None, :, None]
    local_pixels = jnp.pad(own(patches), ((0, 0), (0, padded - patch_count), (0, 0)))
    local_pixels = local_pixels.reshape(rows, -1)

    def embed(patch_full):
        embedded = jnp.dot(local_pixels, patch_full, preferred_element_type=jnp.float32)
        return jnp.where(
            is_class,
            vector_table[final_base + 2],
            jnp.where(
                is_masked, vector_table[final_base + 3], embedded.reshape(images, padded, wide)
            ),
        ).reshape(rows, wide)

    saved_layers = []

    def attention_part(layer_at, state, full):
        normed, residual = state
        base = 6 * layer_at
        projected = low(jnp.dot(normed, full, preferred_element_type=jnp.float32))
        context = attention_forward(projected, bias_grid, images, heads_size, head_width)
        attended = contract_columns(context, full)
        mixed_rows, middle = norm_forward(
            residual, attended, vector_table, base + 3, base + 2, images
        )
        saved_layers.append([residual, normed, projected, context, attended, middle, mixed_rows, full])
        return mixed_rows, middle

    def hidden_part(layer_at, state, up_full, down_full):
        mixed_rows, middle = state
        base = 6 * layer_at
        hidden = jnp.dot(mixed_rows, up_full, preferred_element_type=jnp.float32)
        activated = low(gelu_parts(hidden)[0])
        output = contract_columns(activated, down_full)
        saved_layers[layer_at] += [hidden, activated, output, up_full, down_full]
        return norm_forward(middle, output, vector_table, base + 6, base + 5, images)

    def first_state(patch_full):
        return norm_forward(embed(patch_full), None, vector_table, 0, 0, images)

    if place.short:
        attention_rows = attention_weight.shape[1]
        hidden_rows = hidden_weight.shape[2]
        each = patch_weight.shape[0]
        grown = each + -each % 16
        first = jnp.pad(patch_weight, ((0, grown - each), (0, 0)))
        first = low(jnp.concatenate([attention_weight[0], first], 0))[None]
        source = np.arange(grown)[None, :] + each * np.arange(local_pixels.shape[1] // each)[:, None]
        source = np.where(np.arange(grown)[None, :] < each, source, -1).reshape(-1)
        spread_columns = jnp.asarray(
            np.arange(local_pixels.shape[1])[:, None] == source[None, :], jnp.bfloat16
        )
        layers = [[None, Gather(place, low(hidden_weight[l]))] for l in range(layer_count)]
        for layer_at in range(layer_count):
            shard = low(attention_weight[layer_at])[None] if layer_at else first
            layers[layer_at][0] = Gather(place, shard)
        head_group = Gather(place, low(head_weight)[None])
        token = place.scalars
        turns = tensor_size - 1
        waves = {id(g): turns for pair in layers for g in pair}

        def wave(*groups):
            started = []
            for group in groups:
                if group is not None and waves.get(id(group), 0):
                    waves[id(group)] -= 1
                    group.start("z")
                    started.append((group, "z"))
            return started

        def finish(group, *values):
            while waves.get(id(group), 0):
                values = await_hops(wave(group), *values)
                values = values if isinstance(values, tuple) else (values,)
            return values[0] if len(values) == 1 else values

        def begin(group, *values):
            if group is not None:
                out = lax.optimization_barrier((group.ring[0],) + values)
                group.ring[0], values = out[0], out[1:]
            return values[0] if len(values) == 1 else values

        here, below = layers[0]
        after = layers[1][0] if layer_count > 1 else None
        token = finish(here, token)
        here.start("one")
        token = begin(below, token)
        token, later_bias = lax.optimization_barrier((token, relative_bias))
        bias_grid = bias_expand(later_bias, GRID, padded)
        token = await_hops(wave(below), token)
        token = await_hops(wave(below), token)
        turning = wave(below)
        token = await_hops([(here, "one")], token)
        here.start("two")
        here.start("near")
        token = begin(after, finish(below, token))
        token, bias_grid = await_hops(
            [(here, "two"), (here, "near")] + turning + wave(after), token, bias_grid
        )
        here.start("far")
        below.start("one")
        token = await_hops([(here, "far")] + wave(after), token)
        place.scalars = token
        local_pixels = low(
            jnp.dot(local_pixels, spread_columns, preferred_element_type=jnp.float32)
        )
        patch_full = assemble(place, here, 0, grown, "xycz", "", attention_rows)
        state = first_state(patch_full)
        for layer_at in range(layer_count):
            here, below = layers[layer_at]
            more = layer_at + 1 < layer_count
            ahead, after = layers[layer_at + 1] if more else (head_group, None)
            full = assemble(place, here, 0, attention_rows, "xz", "yc")
            turning = wave(ahead)
            state = attention_part(layer_at, state, full)
            state = await_hops([(below, "one")] + turning, *state)
            below.start("two")
            below.start("near")
            state = begin(after, *state)
            state = await_hops(
                [(below, "two"), (below, "near")] + wave(ahead) + wave(after), *state
            )
            state = finish(ahead, *state)
            below.start("far")
            ahead.start("one")
            turning = wave(after)
            state = await_hops([(below, "far")], *state)
            up_full = assemble(place, below, 0, hidden_rows, "xyc", "z")
            down_full = assemble(place, below, 1, hidden_rows, "xyc", "z")
            state = hidden_part(layer_at, state, up_full, down_full)
            state = await_hops([(ahead, "one")] + turning, *state)
            ahead.start("two")
            ahead.start("near")
            if more:
                state = await_hops([(ahead, "two"), (ahead, "near")] + wave(after), *state)
                state = finish(after, *state)
                after.start("one")
                ahead.start("far")
                following = layers[layer_at + 2][0] if layer_at + 2 < layer_count else None
                state = await_hops([(ahead, "far")] + wave(following), *state)
                state = finish(following, *state)
    else:
        bias_grid = bias_expand(relative_bias, GRID, padded)

        def fetch(shard, row_ways, column_ways):
            full = lax.all_gather(low(shard), axes_of(row_ways), axis=0, tiled=True)
            if column_ways:
                full = lax.all_gather(full, axes_of(column_ways), axis=1, tiled=True)
            return full

        state = first_state(fetch(patch_weight, "xycz", ""))
        for layer_at in range(layer_count):
            full = fetch(attention_weight[layer_at], "xz", "yc")
            state = attention_part(layer_at, state, full)
            up_full = fetch(hidden_weight[layer_at, 0], "xyc", "z")
            down_full = fetch(hidden_weight[layer_at, 1], "xyc", "z")
            state = hidden_part(layer_at, state, up_full, down_full)
        head_full = fetch(head_weight, "xyc", "")
    final_rows, residual = state

    chosen = (jnp.arange(images)[:, None] * padded + own_masked).reshape(-1)
    share = chosen.shape[0]
    choose = (chosen[:, None] == jnp.arange(rows)[None, :]).astype(jnp.bfloat16)
    picked = jnp.dot(choose, final_rows, preferred_element_type=jnp.float32).astype(jnp.bfloat16)
    if place.short:
        rows_ring = place.ring(picked, "z")
        rows_ring[2] = await_hops([(head_group, "two"), (head_group, "near")], rows_ring[2])
        head_group.start("far")
        rows_ring[3:] = [place.hop(rows_ring[2], "z")]
        rows_ring[3] = await_hops([(head_group, "far")], rows_ring[3])
        head_full = assemble(place, head_group, 0, head_weight.shape[0], "xyc", "")
    else:
        rows_ring = place.ring(picked, "z")
    head_rows = jnp.concatenate(rows_ring, 0)
    target_rows = targets.reshape(tensor_size, heads_size, share)
    target_rows = lax.dynamic_index_in_dim(target_rows, heads_index, 1, False)
    target_rows = ordered(place, target_rows, 0, "z").reshape(-1)
    logits = jnp.dot(head_rows, head_full, preferred_element_type=jnp.float32)
    block_width = logits.shape[1]
    onehot = jnp.arange(block_width)[None, :] + tensor_index * block_width == target_rows[:, None]
    local_max = jnp.max(logits, -1)
    local_sum = jnp.sum(jnp.exp(logits - local_max[:, None]), -1)
    local_pick = jnp.sum(jnp.where(onehot, logits, 0.0), -1)

    stats = jnp.stack([local_max, local_sum]).reshape(2, tensor_size, share)

    def turn(value, steps):
        count = tensor_size
        return lax.ppermute(value, "tensor", [(i, (i + steps) % count) for i in range(count)])

    every = [stats]
    for step in range(1, tensor_size):
        every.append(jnp.roll(turn(stats, step), step, 1))
    every = jnp.stack(every)
    score_max = jnp.max(every[:, 0], 0)
    score_sum = jnp.sum(every[:, 1] * jnp.exp(every[:, 0] - score_max), 0)
    log_total = (score_max + jnp.log(score_sum)).reshape(-1)
    loss_part = jnp.sum(log_total[:share]) - jnp.sum(local_pick)
    grad_logits = (
        (jnp.exp(logits - log_total[:, None]) - onehot.astype(jnp.float32)) / total_rows
    ).astype(jnp.bfloat16)
    grad_rows_all = contract_columns(grad_logits, head_full).reshape(tensor_size, share, wide)
    returned = [
        turn(grad_rows_all[step].astype(jnp.bfloat16), tensor_size - step)
        for step in range(1, tensor_size)
    ]
    if returned:
        returned[0], grad_logits = lax.optimization_barrier((returned[0], grad_logits))
    grad_picked = grad_rows_all[0]
    for part in returned:
        grad_picked = grad_picked + part.astype(jnp.float32)
    movers = []

    def send(pairs, row_ways, column_ways):
        packs = [packed_gradient(place, p, row_ways, column_ways) for p in pairs]
        mover = Scatter(place, [p[0] for p in packs], [p[1] for p in packs])
        movers.append(mover)
        return mover

    if place.short:
        head_mover = send([[(head_rows, grad_logits)]], "xyc", "")
    else:
        head_grad = scatter_sum(
            contract_rows(head_rows, grad_logits).reshape(
                sizes["x"], sizes["y"], CORES, -1, block_width
            ),
            "xyc",
        )
    grad_final = lax.dot_general(
        choose.astype(jnp.float32), grad_picked, (((0,), (0,)), ((), ())), precision=highest
    )
    grad_residual, final_sums, grad_output = norm_backward(
        residual, grad_final, None, saved_layers[-1][10], vector_table, final_base, final_base - 1, images
    )
    grad_final_gain, grad_final_shift = final_sums[0], final_sums[1]
    scale_sum = final_sums[2]

    bias_grad = jnp.zeros(bias_grid.shape, jnp.float32)
    layer_grads = [None] * layer_count
    attention_grads = [None] * layer_count
    hidden_grads = [None] * layer_count

    def step(*values):
        return pump(movers, *values) if place.short else (values if len(values) > 1 else values[0])

    def column_blocks(whole, count):
        pieces = whole.reshape(whole.shape[0], count, -1)
        return jnp.stack([pieces[:, i] for i in range(count)])

    for layer_at in reversed(range(layer_count)):
        (residual_in, normed, projected, context, attended, middle, mixed_rows, full) = saved_layers[
            layer_at
        ][:8]
        hidden, activated, output, up_full, down_full = saved_layers[layer_at][8:]
        base = 6 * layer_at
        grad_rows = [None] * 6
        grad_rows[5] = scale_sum
        grad_activated = jnp.dot(grad_output, down_full, preferred_element_type=jnp.float32)
        grad_hidden = low(grad_activated * gelu_parts(hidden)[1])
        grad_hidden = step(grad_hidden)
        if place.short:
            hidden_grads[layer_at] = send(
                [[(mixed_rows, grad_hidden)], [(grad_output, activated)]], "xyc", "z"
            )
        else:
            view = (tensor_size, sizes["x"], sizes["y"], CORES, -1, wide)
            hidden_grads[layer_at] = jnp.stack(
                [
                    scatter_sum(
                        column_blocks(contract_rows(a, b), tensor_size).reshape(
                            view[:-1] + (hidden_weight.shape[3],)
                        ),
                        "zxyc",
                    )
                    for a, b in ((mixed_rows, grad_hidden), (grad_output, activated))
                ]
            )
        grad_mixed = step(contract_columns(grad_hidden, up_full))
        grad_middle, sums, grad_attended = norm_backward(
            middle, grad_mixed, grad_residual, attended, vector_table, base + 3, base + 2, images
        )
        grad_rows[3], grad_rows[4], grad_rows[2] = sums[0], sums[1], sums[2]
        grad_context = low(jnp.dot(grad_attended, full, preferred_element_type=jnp.float32))
        grad_projected, bias_grad = attention_backward(
            projected, grad_context, bias_grid, bias_grad, images, heads_size, head_width
        )
        grad_projected, bias_grad = step(grad_projected, bias_grad)
        pairs = [(normed, grad_projected), (grad_attended, context)]
        if place.short:
            attention_grads[layer_at] = send([pairs], "xz", "yc")
        else:
            whole = sum(contract_rows(a, b) for a, b in pairs)
            attention_grads[layer_at] = scatter_sum(
                column_blocks(whole, heads_size).reshape(
                    sizes["y"], CORES, sizes["x"], tensor_size, -1, attention_weight.shape[2]
                ),
                "ycxz",
            )
        grad_normed = contract_columns(grad_projected, full)
        if place.short and layer_at == 0:
            grad_normed = pump([attention_grads[0]], grad_normed)
        output_below = saved_layers[layer_at - 1][10] if layer_at else None
        grad_residual, sums, *grad_below = norm_backward(
            residual_in, grad_normed, grad_middle, output_below, vector_table, base, base - 1, images
        )
        grad_rows[0], grad_rows[1], scale_sum = sums[0], sums[1], sums[2]
        if layer_at:
            grad_residual, grad_output = step(grad_residual, grad_below[0])
        else:
            grad_residual = step(grad_residual)
        layer_grads[layer_at] = jnp.stack(grad_rows)
    grad_residual = grad_residual.reshape(images, padded, wide)
    held_out = is_masked | (token_ids >= patch_count)[None, :, None]
    grad_embedded = low(jnp.where(held_out, 0.0, grad_residual)).reshape(rows, wide)
    if place.short:
        patch_mover = send([[(local_pixels, grad_embedded)]], "xycz", "")
    else:
        patch_sum = contract_rows(local_pixels, grad_embedded)
    bias_grad, grad_residual = lax.optimization_barrier((bias_grad, grad_residual))
    grad_class = jnp.sum(grad_residual[:, patch_count], 0)
    grad_mask = jnp.sum(jnp.where(is_masked, grad_residual, 0.0), (0, 1))
    vector_grad = jnp.concatenate(
        layer_grads + [jnp.stack([grad_final_gain, grad_final_shift, grad_class, grad_mask])], 0
    )
    collected = step(bias_rows(bias_grad, GRID))
    if place.short:
        for mover in movers:
            if mover.total is not None:
                mover.total, collected = lax.optimization_barrier((mover.total, collected))
    relative_grad = bias_collect(collected, bias_corners(bias_grad, GRID), GRID)

    counts = (1, vector_grad.size, relative_grad.size)
    flat = jnp.concatenate([loss_part.reshape(1), vector_grad.reshape(-1), relative_grad.reshape(-1)])
    flat = jnp.pad(flat, (0, -flat.size % 1024)).reshape(-1, 128)
    if place.short:
        flat = step(flat)
        small = SmallSum(place, flat)
        movers.append(small)
        while any(m.flying for m in movers):
            place.scalars = pump(movers, place.scalars)
        flat = small.total
        patch_grad = patch_mover.total[0][:each]
        head_grad = head_mover.total[0]
        attention_grads = [m.total[0] for m in attention_grads]
        hidden_grads = [m.total for m in hidden_grads]
    else:
        patch_grad = scatter_sum(
            patch_sum.reshape(sizes["x"], sizes["y"], CORES, tensor_size, -1, wide), "xycz"
        )
        flat = lax.psum(flat, ("dp", "heads", "tensor"))
    flat = flat.reshape(-1)
    loss = flat[0] / total_rows
    vector_grad = flat[1 : 1 + counts[1]].reshape(vector_grad.shape)
    relative_grad = flat[1 + counts[1] : sum(counts)].reshape(relative_grad.shape)

    params = (patch_weight, attention_weight, hidden_weight, head_weight, vector_table, relative_bias)
    firsts = (patch_first, attention_first, hidden_first, head_first, vector_first, bias_first)
    seconds = (patch_second, attention_second, hidden_second, head_second, vector_second, bias_second)
    gradients = (
        patch_grad,
        jnp.stack(attention_grads),
        jnp.stack(hidden_grads),
        head_grad,
        vector_grad,
        relative_grad,
    )
    results = [loss]
    for member in range(6):
        results.extend(
            adam_update(
                params[member], firsts[member], seconds[member], gradients[member], learning_rates[member]
            )
        )
    return tuple(results)


def solution(mesh):
    rows_all = P(("dp", "heads", "tensor"), None)
    attention = P(None, ("dp", "tensor"), "heads")
    hidden = P(None, None, ("dp", "heads"), "tensor")
    head = P(("dp", "heads"), "tensor")
    states = (rows_all,) * 3 + (attention,) * 3 + (hidden,) * 3 + (head,) * 3 + (P(),) * 6
    return jax.shard_map(
        shards,
        mesh=mesh,
        in_specs=(P(("dp", "tensor"), None, None), P(("dp", "tensor"), None), P("dp", None)) + states,
        out_specs=(P(),) + states,
        check_vma=False,
    )
```

profile of v0, /device:TPU:0, one launch (start us, length us, event | category | flops | bytes accessed | tf_op | source)
XLA Modules:
  0.0 678.6 jit_solution(14130046995536764802)
XLA Ops:
  6.0 6.8 %collective-permute-done = bf16[1,128,768]{2,1,0:T(8,128)(2,1)S(1)} collective-permute-done((bf16[1,128,768]{2,1,0:T(8,128)(2,1)S(1)}, bf16[1,128,768]{2,1,0:T(8,128)(2,1)S(1)}, u32[]{:S(2)}, u32[]{:S(2)}) %collective-permute-start) | collective-permute-done | bytes 196640 | tf_op jit(solution)/shard_map/ppermute | solution.py:51
  12.8 7.9 %collective-permute-done.1 = bf16[1,128,768]{2,1,0:T(8,128)(2,1)S(1)} collective-permute-done((bf16[1,128,768]{2,1,0:T(8,128)(2,1)S(1)}, bf16[1,128,768]{2,1,0:T(8,128)(2,1)S(1)}, u32[]{:S(2)}, u32[]{:S(2)}) %collective-permute-start.1) | collective-permute-done | bytes 196640 | tf_op jit(solution)/shard_map/ppermute | solution.py:51
  22.1 6.1 collective-permute-done.2
  33.5 8.6 %collective-permute-done.3 = bf16[2,96,768]{2,1,0:T(8,128)(2,1)} collective-permute-done((bf16[2,96,768]{2,1,0:T(8,128)(2,1)S(1)}, bf16[2,96,768]{2,1,0:T(8,128)(2,1)}, u32[]{:S(2)}, u32[]{:S(2)}) %collective-permute-start.3) | collective-permute-done | bytes 294944 | tf_op jit(solution)/shard_map/ppermute | solution.py:51
  42.9 8.1 %collective-permute-done.4 = bf16[2,96,768]{2,1,0:T(8,128)(2,1)} collective-permute-done((bf16[2,96,768]{2,1,0:T(8,128)(2,1)}, bf16[2,96,768]{2,1,0:T(8,128)(2,1)}, u32[]{:S(2)}, u32[]{:S(2)}) %collective-permute-start.4) | collective-permute-done | bytes 294944 | tf_op jit(solution)/shard_map/ppermute | solution.py:51
  91.4 9.5 %shard_map.397.refs_3_ = bf16[416,3072]{1,0:T(8,128)(2,1)S(1)} custom-call(bf16[416,3072]{1,0:T(8,128)(2,1)S(1)} %convolution_convert_fusion.3.block_ref, f32[12,208,208]{2,1,0:T(8,128)S(1)} %shard_map.393.bias_ref), custom_call_target="tpu_custom_call" | custom-call | flops 1 | bytes 1 | tf_op jit(solution)/shard_map/pallas_call | solution.py:729
  110.4 9.2 %collective-permute-done.25 = bf16[2,96,768]{2,1,0:T(8,128)(2,1)S(1)} collective-permute-done((bf16[2,96,768]{2,1,0:T(8,128)(2,1)S(1)}, bf16[2,96,768]{2,1,0:T(8,128)(2,1)S(1)}, u32[]{:S(2)}, u32[]{:S(2)}) %collective-permute-start.25) | collective-permute-done | bytes 294944 | tf_op jit(solution)/shard_map/ppermute | solution.py:51
  160.7 9.5 %shard_map.403.refs_3_ = bf16[416,3072]{1,0:T(8,128)(2,1)S(1)} custom-call(bf16[416,3072]{1,0:T(8,128)(2,1)S(1)} %convolution_convert_fusion.2.block_ref, f32[12,208,208]{2,1,0:T(8,128)S(1)} %shard_map.393.bias_ref), custom_call_target="tpu_custom_call" | custom-call | flops 1 | bytes 1 | tf_op jit(solution)/shard_map/pallas_call | solution.py:729
  175.0 7.7 %collective-permute-done.39.refs_2_ = bf16[4,2,96,768]{3,2,1,0:T(8,128)(2,1)S(1)} collective-permute-done((bf16[4,2,96,768]{3,2,1,0:T(8,128)(2,1)S(1)}, bf16[4,2,96,768]{3,2,1,0:T(8,128)(2,1)S(1)}, u32[]{:S(2)}, u32[]{:S(2)}) %collective-permute-start.39) | collective-permute-done | bytes 1179680 | tf_op jit(solution)/shard_map/ppermute | solution.py:64
  186.9 12.9 %collective-permute-done.41.refs_6_ = bf16[2,2,96,768]{3,2,1,0:T(8,128)(2,1)S(1)} collective-permute-done((bf16[2,2,96,768]{3,2,1,0:T(8,128)(2,1)S(1)}, bf16[2,2,96,768]{3,2,1,0:T(8,128)(2,1)S(1)}, u32[]{:S(2)}, u32[]{:S(2)}) %collective-permute-start.41) | collective-permute-done | bytes 589856 | tf_op jit(solution)/shard_map/ppermute | solution.py:51
  228.5 8.9 %collective-permute-done.50 = bf16[150,768]{1,0:T(8,128)(2,1)} collective-permute-done((bf16[150,768]{1,0:T(8,128)(2,1)S(1)}, bf16[150,768]{1,0:T(8,128)(2,1)}, u32[]{:S(2)}, u32[]{:S(2)}) %collective-permute-start.50) | collective-permute-done | bytes 230432 | tf_op jit(solution)/shard_map/ppermute | solution.py:51
  300.2 7.2 %collective-permute-done.65 = bf16[150,768]{1,0:T(8,128)(2,1)S(1)} collective-permute-done((bf16[150,768]{1,0:T(8,128)(2,1)S(1)}, bf16[150,768]{1,0:T(8,128)(2,1)S(1)}, u32[]{:S(2)}, u32[]{:S(2)}) %collective-permute-start.65) | collective-permute-done | bytes 230432 | tf_op jit(solution)/shard_map/ppermute | solution.py:1034
  307.3 8.9 %collective-permute-done.64 = bf16[150,768]{1,0:T(8,128)(2,1)S(1)} collective-permute-done((bf16[150,768]{1,0:T(8,128)(2,1)S(1)}, bf16[150,768]{1,0:T(8,128)(2,1)S(1)}, u32[]{:S(2)}, u32[]{:S(2)}) %collective-permute-start.64) | collective-permute-done | bytes 230432 | tf_op jit(solution)/shard_map/ppermute | solution.py:1034
  320.6 6.2 shard_map.413
  332.6 6.2 shard_map.412
  363.1 17.5 %shard_map.415 = (bf16[416,3072]{1,0:T(8,128)(2,1)S(1)}, f32[12,208,208]{2,1,0:T(8,128)S(1)}) custom-call(bf16[416,3072]{1,0:T(8,128)(2,1)S(1)} %copy-done.36, bf16[416,3072]{1,0:T(8,128)(2,1)S(1)} %convolution_convert_fusion.1.grad_ref, f32[12,208,208]{2,1,0:T(8,128)S(1)} %copy-done.8, f32[12,208,208]{2,1,0:T(8,128)} %broadcast_in_dim.81.before_ref), custom_call_target="tpu_custom_call" | custom-call | flops 1 | bytes 1 | tf_op jit(solution)/shard_map/pallas_call | solution.py:770
  386.1 10.6 %shard_map.420 = (bf16[2,2,4,96,768]{4,3,2,1,0:T(8,128)(2,1)}, f32[2,2,4,96,768]{4,3,2,1,0:T(8,128)}) custom-call(s32[4]{0:T(128)S(1)} %pad_add_fusion.scalars, bf16[416,768]{1,0:T(8,128)(2,1)S(1)} %copy-done.110, bf16[416,3072]{1,0:T(8,128)(2,1)S(1)} %copy-done.88, bf16[416,768]{1,0:T(8,128)(2,1)S(1)} %get-tuple-element.377.refs_2_, ...), custom_call_target="tpu_custom_call" | custom-call | flops 1 | bytes 1 | tf_op jit(solution)/shard_map/pallas_call | solution.py:415
  410.2 20.6 %collective-permute-done.75.refs_4_ = bf16[2,4,96,768]{3,2,1,0:T(8,128)(2,1)S(1)} collective-permute-done((bf16[2,4,96,768]{3,2,1,0:T(8,128)(2,1)S(1)}, bf16[2,4,96,768]{3,2,1,0:T(8,128)(2,1)S(1)}, u32[]{:S(2)}, u32[]{:S(2)}) %collective-permute-start.75) | collective-permute-done | bytes 1179680 | tf_op jit(solution)/shard_map/ppermute | solution.py:51
  441.5 8.0 %fusion.11.refs_1_ = bf16[416,3072]{1,0:T(8,128)(2,1)} fusion(f32[416,3072]{1,0:T(8,128)} %get-tuple-element.540, bf16[416,768]{1,0:T(8,128)(2,1)S(1)} %get-tuple-element.399.refs_0_, bf16[768,3072]{1,0:T(8,128)(2,1)} %copy-done.65), kind=kOutput, calls=%fused_computation.15 | convolution fusion | flops 1975713792 | bytes 13025280 | tf_op jit(solution)/shard_map/dot_general | solution.py:1103
  450.6 6.2 shard_map.425
  459.6 6.2 shard_map.424
  480.5 6.6 collective-permute-done.82.refs_2_
  504.8 17.5 %shard_map.427 = (bf16[416,3072]{1,0:T(8,128)(2,1)S(1)}, f32[12,208,208]{2,1,0:T(8,128)S(1)}) custom-call(bf16[416,3072]{1,0:T(8,128)(2,1)S(1)} %copy-done.34, bf16[416,3072]{1,0:T(8,128)(2,1)S(1)} %convolution_convert_fusion.grad_ref, f32[12,208,208]{2,1,0:T(8,128)S(1)} %copy-done.9, f32[12,208,208]{2,1,0:T(8,128)} %copy-done.84), custom_call_target="tpu_custom_call" | custom-call | flops 1 | bytes 1 | tf_op jit(solution)/shard_map/pallas_call | solution.py:770
  524.8 10.4 %shard_map.430 = (bf16[2,2,4,96,768]{4,3,2,1,0:T(8,128)(2,1)}, f32[2,2,4,96,768]{4,3,2,1,0:T(8,128)}) custom-call(s32[4]{0:T(128)S(1)} %pad_add_fusion.scalars, bf16[416,768]{1,0:T(8,128)(2,1)S(1)} %copy-done.91, bf16[416,3072]{1,0:T(8,128)(2,1)S(1)} %get-tuple-element.429.refs_1_, bf16[416,768]{1,0:T(8,128)(2,1)S(1)} %get-tuple-element.416.refs_2_, ...), custom_call_target="tpu_custom_call" | custom-call | flops 1 | bytes 1 | tf_op jit(solution)/shard_map/pallas_call | solution.py:415
  (823 shorter events, 444.4 us)
Async XLA Ops:
  33.5 23.8 %collective-permute-start.9 = (bf16[4,1,128,768]{3,2,1,0:T(8,128)(2,1)S(1)}, bf16[4,1,128,768]{3,2,1,0:T(8,128)(2,1)}, u32[]{:S(2)}, u32[]{:S(2)}) collective-permute-start(bf16[4,1,128,768]{3,2,1,0:T(8,128)(2,1)S(1)} %pad_maximum_fusion.4.refs_0_), channel_id=1, source_target_pairs={{0,4},{4,0},{8,12},{12,8},{1,5},{5,1},{9,13},{13,9},{2,6},{6,2},{1... | collective-permute-start | bytes 2359304 | tf_op jit(solution)/shard_map/ppermute | solution.py:64
  78.3 28.0 %collective-permute-start.17 = (bf16[4,2,96,768]{3,2,1,0:T(8,128)(2,1)S(1)}, bf16[4,2,96,768]{3,2,1,0:T(8,128)(2,1)S(1)}, u32[]{:S(2)}, u32[]{:S(2)}) collective-permute-start(bf16[4,2,96,768]{3,2,1,0:T(8,128)(2,1)S(1)} %pad_maximum_fusion.refs_0_), channel_id=1, source_target_pairs={{0,8},{4,12},{8,0},{12,4},{1,9},{5,13},{9,1},{13,5},{2,10},{6,14},... | collective-permute-start | bytes 3538952 | tf_op jit(solution)/shard_map/ppermute | solution.py:64
  78.9 27.7 %collective-permute-start.18 = (bf16[4,2,96,768]{3,2,1,0:T(8,128)(2,1)S(1)}, bf16[4,2,96,768]{3,2,1,0:T(8,128)(2,1)S(1)}, u32[]{:S(2)}, u32[]{:S(2)}) collective-permute-start(bf16[4,2,96,768]{3,2,1,0:T(8,128)(2,1)S(1)} %pad_maximum_fusion.refs_0_), channel_id=1, source_target_pairs={{0,16},{16,0},{1,17},{17,1},{2,18},{18,2},{3,19},{19,3},{4,20},{20... | collective-permute-start | bytes 3538952 | tf_op jit(solution)/shard_map/ppermute | solution.py:51
  84.1 25.2 %collective-permute-start.22 = (bf16[4,2,96,768]{3,2,1,0:T(8,128)(2,1)S(1)}, bf16[4,2,96,768]{3,2,1,0:T(8,128)(2,1)S(1)}, u32[]{:S(2)}, u32[]{:S(2)}) collective-permute-start(bf16[4,2,96,768]{3,2,1,0:T(8,128)(2,1)S(1)} %pad_maximum_fusion.refs_0_), channel_id=1, source_target_pairs={{0,4},{4,0},{8,12},{12,8},{1,5},{5,1},{9,13},{13,9},{2,6},{6,2},{1... | collective-permute-start | bytes 3538952 | tf_op jit(solution)/shard_map/ppermute | solution.py:64
  154.7 28.0 %collective-permute-start.39 = (bf16[4,2,96,768]{3,2,1,0:T(8,128)(2,1)S(1)}, bf16[4,2,96,768]{3,2,1,0:T(8,128)(2,1)S(1)}, u32[]{:S(2)}, u32[]{:S(2)}) collective-permute-start(bf16[4,2,96,768]{3,2,1,0:T(8,128)(2,1)S(1)} %pad_maximum_fusion.1.refs_0_), channel_id=1, source_target_pairs={{0,8},{4,12},{8,0},{12,4},{1,9},{5,13},{9,1},{13,5},{2,10},{6,14},... | collective-permute-start | bytes 3538952 | tf_op jit(solution)/shard_map/ppermute | solution.py:64
  156.3 27.7 %collective-permute-start.40 = (bf16[4,2,96,768]{3,2,1,0:T(8,128)(2,1)S(1)}, bf16[4,2,96,768]{3,2,1,0:T(8,128)(2,1)S(1)}, u32[]{:S(2)}, u32[]{:S(2)}) collective-permute-start(bf16[4,2,96,768]{3,2,1,0:T(8,128)(2,1)S(1)} %pad_maximum_fusion.1.refs_0_), channel_id=1, source_target_pairs={{0,16},{16,0},{1,17},{17,1},{2,18},{18,2},{3,19},{19,3},{4,20},{20... | collective-permute-start | bytes 3538952 | tf_op jit(solution)/shard_map/ppermute | solution.py:51
  160.6 25.3 %collective-permute-start.43 = (bf16[4,2,96,768]{3,2,1,0:T(8,128)(2,1)S(1)}, bf16[4,2,96,768]{3,2,1,0:T(8,128)(2,1)S(1)}, u32[]{:S(2)}, u32[]{:S(2)}) collective-permute-start(bf16[4,2,96,768]{3,2,1,0:T(8,128)(2,1)S(1)} %pad_maximum_fusion.1.refs_0_), channel_id=1, source_target_pairs={{0,4},{4,0},{8,12},{12,8},{1,5},{5,1},{9,13},{13,9},{2,6},{6,2},{1... | collective-permute-start | bytes 3538952 | tf_op jit(solution)/shard_map/ppermute | solution.py:64
  205.6 36.0 %collective-permute-start.54 = (bf16[1,1,96,2048]{3,2,1,0:T(8,128)(2,1)}, bf16[1,1,96,2048]{3,2,1,0:T(8,128)(2,1)}, u32[]{:S(2)}, u32[]{:S(2)}) collective-permute-start(bf16[1,1,96,2048]{3,2,1,0:T(8,128)(2,1)} %convert_bitcast_fusion.refs_0_), channel_id=1, source_target_pairs={{0,4},{4,0},{8,12},{12,8},{1,5},{5,1},{9,13},{13,9},{2,6},{6,2},{1... | collective-permute-start | bytes 1179656 | tf_op jit(solution)/shard_map/ppermute | solution.py:64
  296.6 36.0 %collective-permute-start.66 = (bf16[2,2,1,96,2048]{4,3,2,1,0:T(8,128)(2,1)S(1)}, bf16[2,2,1,96,2048]{4,3,2,1,0:T(8,128)(2,1)S(1)}, u32[]{:S(2)}, u32[]{:S(2)}) collective-permute-start(bf16[2,2,1,96,2048]{4,3,2,1,0:T(8,128)(2,1)S(1)} %get-tuple-element.367), channel_id=1, source_target_pairs={{0,4},{4,0},{8,12},{12,8},{1,5},{5,1},{9,13},{13,9},{2,6},{6,2},{1... | collective-permute-start | bytes 4718600 | tf_op jit(solution)/shard_map/ppermute | solution.py:64
  351.9 32.4 %collective-permute-start.73 = (bf16[2,2,96,768]{3,2,1,0:T(8,128)(2,1)}, bf16[2,2,96,768]{3,2,1,0:T(8,128)(2,1)}, u32[]{:S(2)}, u32[]{:S(2)}) collective-permute-start(bf16[2,2,96,768]{3,2,1,0:T(8,128)(2,1)} %get-tuple-element.388), channel_id=1, source_target_pairs={{0,8},{4,12},{8,0},{12,4},{1,9},{5,13},{9,1},{13,5},{2,10},{6,14},... | collective-permute-start | bytes 1769480 | tf_op jit(solution)/shard_map/ppermute | solution.py:64
  352.4 31.9 %collective-permute-start.74 = (bf16[2,2,96,768]{3,2,1,0:T(8,128)(2,1)}, bf16[2,2,96,768]{3,2,1,0:T(8,128)(2,1)}, u32[]{:S(2)}, u32[]{:S(2)}) collective-permute-start(bf16[2,2,96,768]{3,2,1,0:T(8,128)(2,1)} %get-tuple-element.389), channel_id=1, source_target_pairs={{0,16},{16,0},{1,17},{17,1},{2,18},{18,2},{3,19},{19,3},{4,20},{20... | collective-permute-start | bytes 1769480 | tf_op jit(solution)/shard_map/ppermute | solution.py:51
  354.6 28.9 %collective-permute-start.71 = (bf16[1,2,48,2048]{3,2,1,0:T(8,128)(2,1)}, bf16[1,2,48,2048]{3,2,1,0:T(8,128)(2,1)S(1)}, u32[]{:S(2)}, u32[]{:S(2)}) collective-permute-start(bf16[1,2,48,2048]{3,2,1,0:T(8,128)(2,1)} %get-tuple-element.382), channel_id=1, source_target_pairs={{0,16},{16,0},{1,17},{17,1},{2,18},{18,2},{3,19},{19,3},{4,20},{20... | collective-permute-start | bytes 1179656 | tf_op jit(solution)/shard_map/ppermute | solution.py:51
  355.4 28.9 %collective-permute-start.72 = (bf16[1,2,48,2048]{3,2,1,0:T(8,128)(2,1)}, bf16[1,2,48,2048]{3,2,1,0:T(8,128)(2,1)}, u32[]{:S(2)}, u32[]{:S(2)}) collective-permute-start(bf16[1,2,48,2048]{3,2,1,0:T(8,128)(2,1)} %get-tuple-element.383), channel_id=1, source_target_pairs={{0,8},{4,12},{8,0},{12,4},{1,9},{5,13},{9,1},{13,5},{2,10},{6,14},... | collective-permute-start | bytes 1179656 | tf_op jit(solution)/shard_map/ppermute | solution.py:64
  396.6 35.2 %collective-permute-start.77 = (bf16[2,2,4,96,768]{4,3,2,1,0:T(8,128)(2,1)}, bf16[2,2,4,96,768]{4,3,2,1,0:T(8,128)(2,1)S(1)}, u32[]{:S(2)}, u32[]{:S(2)}) collective-permute-start(bf16[2,2,4,96,768]{4,3,2,1,0:T(8,128)(2,1)} %get-tuple-element.398), channel_id=1, source_target_pairs={{0,4},{4,0},{8,12},{12,8},{1,5},{5,1},{9,13},{13,9},{2,6},{6,2},{1... | collective-permute-start | bytes 7077896 | tf_op jit(solution)/shard_map/ppermute | solution.py:64
  402.4 28.4 %collective-permute-start.75 = (bf16[2,4,96,768]{3,2,1,0:T(8,128)(2,1)S(1)}, bf16[2,4,96,768]{3,2,1,0:T(8,128)(2,1)S(1)}, u32[]{:S(2)}, u32[]{:S(2)}) collective-permute-start(bf16[2,4,96,768]{3,2,1,0:T(8,128)(2,1)S(1)} %get-tuple-element.396), channel_id=1, source_target_pairs={{0,16},{16,0},{1,17},{17,1},{2,18},{18,2},{3,19},{19,3},{4,20},{20... | collective-permute-start | bytes 3538952 | tf_op jit(solution)/shard_map/ppermute | solution.py:51
  403.8 28.1 %collective-permute-start.76 = (bf16[2,4,96,768]{3,2,1,0:T(8,128)(2,1)S(1)}, bf16[2,4,96,768]{3,2,1,0:T(8,128)(2,1)S(1)}, u32[]{:S(2)}, u32[]{:S(2)}) collective-permute-start(bf16[2,4,96,768]{3,2,1,0:T(8,128)(2,1)S(1)} %get-tuple-element.397), channel_id=1, source_target_pairs={{0,8},{4,12},{8,0},{12,4},{1,9},{5,13},{9,1},{13,5},{2,10},{6,14},... | collective-permute-start | bytes 3538952 | tf_op jit(solution)/shard_map/ppermute | solution.py:64
  456.8 31.4 %collective-permute-start.85 = (bf16[2,2,4,96,768]{4,3,2,1,0:T(8,128)(2,1)}, bf16[2,2,4,96,768]{4,3,2,1,0:T(8,128)(2,1)S(1)}, u32[]{:S(2)}, u32[]{:S(2)}) collective-permute-start(bf16[2,2,4,96,768]{4,3,2,1,0:T(8,128)(2,1)} %get-tuple-element.413), channel_id=1, source_target_pairs={{0,4},{4,0},{8,12},{12,8},{1,5},{5,1},{9,13},{13,9},{2,6},{6,2},{1... | collective-permute-start | bytes 7077896 | tf_op jit(solution)/shard_map/ppermute | solution.py:64
  489.2 34.7 %collective-permute-start.86 = (bf16[2,96,768]{2,1,0:T(8,128)(2,1)}, bf16[2,96,768]{2,1,0:T(8,128)(2,1)S(1)}, u32[]{:S(2)}, u32[]{:S(2)}) collective-permute-start(bf16[2,96,768]{2,1,0:T(8,128)(2,1)} %fusion.26), channel_id=1, source_target_pairs={{0,1},{1,2},{2,3},{3,0},{4,5},{5,6},{6,7},{7,4},{8,9},{9,10},{10,1... | collective-permute-start | bytes 884744 | tf_op jit(solution)/shard_map/ppermute | solution.py:51
  492.6 31.2 %collective-permute-start.88 = (bf16[2,2,96,768]{3,2,1,0:T(8,128)(2,1)}, bf16[2,2,96,768]{3,2,1,0:T(8,128)(2,1)S(1)}, u32[]{:S(2)}, u32[]{:S(2)}) collective-permute-start(bf16[2,2,96,768]{3,2,1,0:T(8,128)(2,1)} %get-tuple-element.427), channel_id=1, source_target_pairs={{0,8},{4,12},{8,0},{12,4},{1,9},{5,13},{9,1},{13,5},{2,10},{6,14},... | collective-permute-start | bytes 1769480 | tf_op jit(solution)/shard_map/ppermute | solution.py:64
  494.2 30.5 %collective-permute-start.89 = (bf16[2,2,96,768]{3,2,1,0:T(8,128)(2,1)S(1)}, bf16[2,2,96,768]{3,2,1,0:T(8,128)(2,1)S(1)}, u32[]{:S(2)}, u32[]{:S(2)}) collective-permute-start(bf16[2,2,96,768]{3,2,1,0:T(8,128)(2,1)S(1)} %get-tuple-element.428), channel_id=1, source_target_pairs={{0,16},{16,0},{1,17},{17,1},{2,18},{18,2},{3,19},{19,3},{4,20},{20... | collective-permute-start | bytes 1769480 | tf_op jit(solution)/shard_map/ppermute | solution.py:51
  496.8 27.0 %collective-permute-start.87 = (bf16[1,96,768]{2,1,0:T(8,128)(2,1)S(1)}, bf16[1,96,768]{2,1,0:T(8,128)(2,1)S(1)}, u32[]{:S(2)}, u32[]{:S(2)}) collective-permute-start(bf16[1,96,768]{2,1,0:T(8,128)(2,1)S(1)} %fusion.55), channel_id=1, source_target_pairs={{0,1},{1,2},{2,3},{3,0},{4,5},{5,6},{6,7},{7,4},{8,9},{9,10},{10,1... | collective-permute-start | bytes 442376 | tf_op jit(solution)/shard_map/ppermute | solution.py:51
  535.2 27.3 %collective-permute-start.90 = (bf16[2,2,4,96,768]{4,3,2,1,0:T(8,128)(2,1)}, bf16[2,2,4,96,768]{4,3,2,1,0:T(8,128)(2,1)}, u32[]{:S(2)}, u32[]{:S(2)}) collective-permute-start(bf16[2,2,4,96,768]{4,3,2,1,0:T(8,128)(2,1)} %get-tuple-element.430), channel_id=1, source_target_pairs={{0,4},{4,0},{8,12},{12,8},{1,5},{5,1},{9,13},{13,9},{2,6},{6,2},{1... | collective-permute-start | bytes 7077896 | tf_op jit(solution)/shard_map/ppermute | solution.py:64
  547.9 29.1 %collective-permute-start.92 = (bf16[2,4,96,768]{3,2,1,0:T(8,128)(2,1)}, bf16[2,4,96,768]{3,2,1,0:T(8,128)(2,1)}, u32[]{:S(2)}, u32[]{:S(2)}) collective-permute-start(bf16[2,4,96,768]{3,2,1,0:T(8,128)(2,1)} %get-tuple-element.443), channel_id=1, source_target_pairs={{0,16},{16,0},{1,17},{17,1},{2,18},{18,2},{3,19},{19,3},{4,20},{20... | collective-permute-start | bytes 3538952 | tf_op jit(solution)/shard_map/ppermute | solution.py:51
  549.0 29.1 %collective-permute-start.93 = (bf16[2,4,96,768]{3,2,1,0:T(8,128)(2,1)}, bf16[2,4,96,768]{3,2,1,0:T(8,128)(2,1)}, u32[]{:S(2)}, u32[]{:S(2)}) collective-permute-start(bf16[2,4,96,768]{3,2,1,0:T(8,128)(2,1)} %get-tuple-element.444), channel_id=1, source_target_pairs={{0,8},{4,12},{8,0},{12,4},{1,9},{5,13},{9,1},{13,5},{2,10},{6,14},... | collective-permute-start | bytes 3538952 | tf_op jit(solution)/shard_map/ppermute | solution.py:64
  (286 other events, 2626.3 us)
where the time goes:
time: 688 us; the launch traced here: 679 us
  waiting for transfers between devices  202 us (29%)
  Pallas kernels  174 us (25%)
  starting transfers between devices  89.9 us (13%)
  local copies, waits for them, and re-layouts  88.4 us (13%)
  matrix products  75.1 us (11%)
  other arithmetic  42.3 us (6%)
    ppermute x53, waiting for transfers between devices, hop(): lax.ppermute(value, axis, [(i, (i + 1) % count) for i in range(count)])  148 us
    unnamed x386, local copies, waits for them, and re-layouts  57.9 us
    pallas_call x8, Pallas kernels, packed_gradient(): pl.pallas_call(body, out_shape=(jax.ShapeDtypeStruct(shape, jnp.bfloat16)...  53.7 us
    ppermute x53, starting transfers between devices, hop(): lax.ppermute(value, axis, [(i, (i + 1) % count) for i in range(count)])  48.6 us
    pallas_call x2, Pallas kernels, attention_backward(): pl.pallas_call(body, out_shape=(jax.ShapeDtypeStruct((rows, total), jnp.b...  35 us
    pallas_call x18, Pallas kernels, merged(): pl.pallas_call(body, out_shape=shapes, grid=(depth,), in_specs=blocks, ou...  33.6 us
    ppermute x57, starting transfers between devices, hop(): return lax.ppermute(value, 'heads', pairs)  30.5 us
    dot_general x9, matrix products, contract_columns(): lax.dot_general(left_side, right_side, (((1,), (1,)), ((), ())), preferre...  30 us
  transfers between devices with their start and end apart: 119, of which 55 were waited for; matrix products, arithmetic and copies ran while one was open for 16% of the time, Pallas kernels for 20%

commit v1 on v0

--- a/solution.py
+++ b/solution.py
@@ -62,6 +62,26 @@
                 for c in range(CORES)
             ]
         return lax.ppermute(value, "heads", pairs)
+
+    def turn(self, value, steps):
+        count = self.size["z"]
+        pairs = [(i, (i + steps) % count) for i in range(count)]
+        return lax.ppermute(value, "tensor", pairs)
+
+    def across(self, value):
+        x, y = self.size["x"], self.size["y"]
+        pairs = [
+            ((i * y + j) * CORES + c, ((i + 1) % x * y + (j + 1) % y) * CORES + c)
+            for i in range(x)
+            for j in range(y)
+            for c in range(CORES)
+        ]
+        return lax.ppermute(value, ("dp", "heads"), pairs)
+
+    def send(self, value, way):
+        if isinstance(way, int):
+            return self.turn(value, way)
+        return self.across(value) if way == "xy" else self.hop(value, way)
 
     def ring(self, value, way):
         held = [value]
@@ -128,17 +148,16 @@
 
 
 def merged(kept, arrived, keys, halves, whole, out_type):
-    count, depth = len(kept), kept[0].shape[2]
-    r, c = kept[0].shape[3:]
+    count, (depth, r, c) = len(kept), kept[0][0, 0].shape
     half = depth // 2
     split = out_type == "split"
     kind = jnp.float32 if out_type == "own" else jnp.bfloat16
     blocks, operands, kinds = [], [], []
     for key in keys:
         for m in range(count):
-            for source in (kept[m], arrived[m]):
-                blocks.append(pl.BlockSpec((1, 1, 1, r, c), lambda i, k=key: (*k, i, 0, 0)))
-                operands.append(source)
+            blocks.append(pl.BlockSpec((1, r, c), lambda i: (i, 0, 0)))
+            blocks.append(pl.BlockSpec((1, 1, 1, r, c), lambda i, k=key: (*k, i, 0, 0)))
+            operands += [kept[m][key], arrived[m]]
     low_map = lambda i: (0, jnp.minimum(i, half - 1), 0, 0)
     high_map = lambda i: (0, jnp.maximum(i - half, 0), 0, 0)
     for side in halves:
@@ -161,7 +180,7 @@
         for n in range(len(keys)):
             for m in range(count):
                 at = 2 * (n * count + m)
-                total = ins[at][0, 0, 0] + ins[at + 1][0, 0, 0].astype(jnp.float32)
+                total = ins[at][0] + ins[at + 1][0, 0, 0].astype(jnp.float32)
                 for extra in ins[base + len(halves) :]:
                     total = total + extra[m, 0].astype(jnp.float32)
                 if split:
@@ -193,71 +212,99 @@
     def __init__(self, place, sent, kept):
         self.place, self.state, self.total = place, "c", None
         self.flying = [place.hop(s, "c") for s in sent]
-        self.kept, self.depth = kept, kept[0].shape[2]
+        self.kept, self.depth = kept, kept[0][0, 0].shape[0]
+        self.rider = None
 
     def view(self, values):
         if self.depth > 1:
             return values
-        return [v.reshape(v.shape[:2] + (2, v.shape[3] // 2, v.shape[4])) for v in values]
+        cut = lambda v: v.reshape(v.shape[:-3] + (2, v.shape[-2] // 2, v.shape[-1]))
+        return [jax.tree.map(cut, v) for v in values]
 
     def land(self, values):
-        place, self.flying = self.place, []
+        self.flying = []
         if self.state == "c":
             self.kept, self.near = self.view(self.kept), self.view(values)
             low, high = merged(self.kept, self.near, [(1, 1)], [], [], "split")
-            self.flying = [place.hop(low, "y"), place.hop(high, "x")]
             self.state = "two"
-        elif self.state == "two":
+            return [(low, "y"), (high, "x")]
+        if self.state == "two":
             x, y = merged(
                 self.kept, self.near, [(1, 0), (0, 1)], [(0, values[0]), (1, values[1])], [], "low"
             )
-            self.flying = [place.hop(x, "x"), place.hop(y, "y")]
             self.state = "one"
-        elif self.state == "one":
+            return [(x, "x"), (y, "y")]
+        if self.state == "one":
             (self.own,) = merged(self.kept, self.near, [(0, 0)], [], list(values), "own")
             if self.depth == 1:
                 shape = self.own.shape
                 self.total = self.own.reshape(shape[0], 2 * shape[2], shape[3])
-                self.state = "done"
-            else:
-                self.flying = [place.hop(self.own[:, 1].astype(jnp.bfloat16), "z")]
-                self.step, self.state = 2, "z"
-        else:
-            running = values[0].astype(jnp.float32) + self.own[:, self.step % self.depth]
-            if self.step % self.depth:
-                self.flying = [place.hop(running.astype(jnp.bfloat16), "z")]
-                self.step += 1
-            else:
-                self.total, self.state = running, "done"
+                return []
+            self.state = "z"
+            if self.rider is not None:
+                self.own = jnp.concatenate([self.own, self.rider.own[None]], 2)
+                return around(self.own, 1)
+            self.turns = 1
+            return [(self.own[:, 1].astype(jnp.bfloat16), 1)]
+        if self.rider is None:
+            self.turns += 1
+            running = values[0].astype(jnp.float32) + self.own[:, self.turns % self.depth]
+            if self.turns % self.depth:
+                return [(running.astype(jnp.bfloat16), 1)]
+            self.total = running
+            return []
+        self.total = self.own[:, 0]
+        for value in values:
+            self.total = self.total + value.astype(jnp.float32)
+        height = self.total.shape[1] - self.rider.own.shape[1]
+        self.total, self.rider.total = self.total[:, :height], self.total[0, height:]
+        return []
+
+
+def around(value, dim):
+    count = value.shape[dim]
+    return [
+        (lax.index_in_dim(value, k, dim, False).astype(jnp.bfloat16), count - k)
+        for k in range(1, count)
+    ]
+
+
+class Brief:
+    def __init__(self, place, sent, kept):
+        self.place, self.state, self.total = place, "c", None
+        self.flying, self.kept = [place.hop(sent, "c")], kept
+
+    def land(self, values):
+        self.flying = []
+        if self.state == "c":
+            add = lambda at: self.kept[at] + values[0][at].astype(jnp.float32)
+            self.own, self.state = add((0, 0)), "xy"
+            ways = (((1, 0), "x"), ((0, 1), "y"), ((1, 1), "xy"))
+            return [(add(at).astype(jnp.bfloat16), way) for at, way in ways]
+        for value in values:
+            self.own = self.own + value.astype(jnp.float32)
+        return []
 
 
 class SmallSum:
     def __init__(self, place, value):
-        self.place, self.ways, self.total = place, list("cxyz"), None
-        self.send(value)
-
-    def send(self, value):
-        self.own, self.state = value, self.ways.pop(0)
-        count = self.place.size[self.state]
-        if self.state == "z":
-            self.flying = [
-                lax.ppermute(value, "tensor", [(i, (i + k) % count) for i in range(count)])
-                for k in range(1, count)
-            ]
-        else:
-            self.flying = [self.place.hop(value, self.state)]
+        self.place, self.state, self.total = place, "c", None
+        self.own, self.flying = value, [place.hop(value, "c")]
 
     def land(self, values):
-        self.flying, held = [], jnp.stack([self.own, *values])
-        if len(values) > 1:
-            held = ordered(self.place, held, 0, self.state)
-        total = held[0]
+        self.flying = []
+        if self.state == "c":
+            self.own, self.state = self.own + values[0], "xy"
+            return [(self.own, way) for way in ("x", "y", "xy")]
+        if self.state == "xy":
+            x, y, xy = values
+            self.own, self.state = (self.own + x) + (y + xy), "z"
+            return [(self.own, k) for k in range(1, self.place.size["z"])]
+        held = ordered(self.place, jnp.stack([self.own, *values]), 0, "z")
+        self.total = held[0]
         for entry in range(1, held.shape[0]):
-            total = total + held[entry]
-        if self.ways:
-            self.send(total)
-        else:
-            self.total = total
+            self.total = self.total + held[entry]
+        return []
 
 
 def await_hops(waited, *values):
@@ -274,10 +321,15 @@
     active = [m for m in movers if m.flying]
     loads = [m.flying for m in active]
     out = lax.optimization_barrier(tuple(values) + tuple(v for load in loads for v in load))
-    at = len(values)
+    at, nexts = len(values), []
     for mover, load in zip(active, loads, strict=True):
-        mover.land(out[at : at + len(load)])
+        nexts += [(mover, *n) for n in mover.land(out[at : at + len(load)])]
         at += len(load)
+    if nexts:
+        ready = lax.optimization_barrier(out[: len(values)] + tuple(n[1] for n in nexts))
+        out = ready[: len(values)]
+        for (mover, _, way), value in zip(nexts, ready[len(values) :], strict=True):
+            mover.flying.append(mover.place.send(value, way))
     return out[0] if len(values) == 1 else out[: len(values)]
 
 
@@ -361,8 +413,9 @@
 
     def body(scalars, *refs):
         ins = refs[: 2 * len(pairs)]
-        sent, kept, work = refs[2 * len(pairs) : 2 * len(pairs) + 3]
-        turned = refs[2 * len(pairs) + 3 :]
+        sent = refs[2 * len(pairs)]
+        kept = dict(zip(quarters, refs[2 * len(pairs) + 1 :]))
+        work, *turned = refs[2 * len(pairs) + 1 + len(quarters) :]
         step = pl.program_id(0)
 
         @pl.when(step == 0)
@@ -385,9 +438,19 @@
                 if "c" in ks and ks["c"] != kc:
                     continue
                 start = pl.multiple_of(owner(scalars, sizes, row_ways, ks) * r, r)
-                block = work[pl.ds(start, r), :].astype(out.dtype)
+                block = work[pl.ds(start, r), :]
                 at = (ks["x"], 0 if by_core else ks["y"], ks.get("z", 0))
-                out[at] = block
+                if kc:
+                    out[at] = block.astype(jnp.bfloat16)
+                elif by_core:
+                    for ky in range(sizes["y"]):
+
+                        @pl.when(step == sizes["y"] + ky)
+                        def _(ky=ky, block=block):
+                            kept[ks["x"], ky][at[2]] = block
+
+                else:
+                    kept[at[:2]][at[2]] = block
 
         if by_core:
             pl.when(step < sizes["y"])(lambda: place_blocks(sent, 1))
@@ -400,11 +463,13 @@
         block = (sizes["x"], 1, depth, r, c)
         last = sizes["y"] - 1
         sent_map = lambda i, s: (0, jnp.minimum(i, last), 0, 0, 0)
-        kept_map = lambda i, s: (0, jnp.maximum(i - last - 1, 0), 0, 0, 0)
+        kept_block, kept_map = (depth, r, c), lambda i, s: (0, 0, 0)
     else:
         block = (sizes["x"], sizes["y"], depth if by_rows else 1, r, c)
-        sent_map = kept_map = lambda i, s: (0, 0, i, 0, 0)
+        sent_map = lambda i, s: (0, 0, i, 0, 0)
+        kept_block, kept_map = block[2:], lambda i, s: (i, 0, 0)
     shape = (sizes["x"], sizes["y"], depth, r, c)
+    quarters = list(np.ndindex(sizes["x"], sizes["y"]))
     in_specs, operands = [], []
     for left, right in pairs:
         in_specs += [
@@ -412,23 +477,23 @@
             pl.BlockSpec((tokens, c), lambda i, s: (0, column_of(i, s))),
         ]
         operands += [left, right]
-    return pl.pallas_call(
+    sent, *kept = pl.pallas_call(
         body,
-        out_shape=(
-            jax.ShapeDtypeStruct(shape, jnp.bfloat16),
-            jax.ShapeDtypeStruct(shape, jnp.float32),
-        ),
+        out_shape=[jax.ShapeDtypeStruct(shape, jnp.bfloat16)]
+        + [jax.ShapeDtypeStruct(shape[2:], jnp.float32)] * len(quarters),
         grid_spec=pltpu.PrefetchScalarGridSpec(
             num_scalar_prefetch=1,
             grid=(len(steps),),
             in_specs=in_specs,
-            out_specs=(pl.BlockSpec(block, sent_map), pl.BlockSpec(block, kept_map)),
+            out_specs=[pl.BlockSpec(block, sent_map)]
+            + [pl.BlockSpec(kept_block, kept_map)] * len(quarters),
             scratch_shapes=[pltpu.VMEM((wide, c), jnp.float32)]
             + [pltpu.VMEM((wide, tokens), jnp.bfloat16) for _ in pairs],
         ),
         compiler_params=pltpu.CompilerParams(vmem_limit_bytes=48 * 2**20),
         cost_estimate=LIGHT,
     )(place.scalars, *operands)
+    return sent, dict(zip(quarters, kept))
 
 
 AXES = {"x": ("dp",), "yc": ("heads",), "z": ("tensor",)}
@@ -695,42 +760,60 @@
     )
 
 
-def heads_of(block, width):
-    scale = width ** (-0.5)
-    for at in range(0, 3 * block.shape[1] // 4, 3 * width):
-        query = block[:, at : at + width].astype(jnp.float32) * scale
-        yield (
-            query.astype(jnp.bfloat16),
-            block[:, at + width : at + 2 * width],
-            block[:, at + 2 * width : at + 3 * width],
-        )
+def batch_columns(left_side, right_side):
+    return lax.dot_general(
+        left_side, right_side, (((2,), (2,)), ((0,), (0,))), preferred_element_type=jnp.float32
+    )
+
+
+def batch_rows(left_side, right_side):
+    return lax.dot_general(
+        left_side, right_side, (((1,), (1,)), ((0,), (0,))), preferred_element_type=jnp.float32
+    )
+
+
+def batch_matmul(left_side, right_side):
+    return lax.dot_general(
+        left_side, right_side, (((2,), (1,)), ((0,), (0,))), preferred_element_type=jnp.float32
+    )
+
+
+def heads_of(block, count, width):
+    parts = [
+        jnp.stack([block[:, (3 * j + i) * width : (3 * j + i + 1) * width] for j in range(count)])
+        for i in range(3)
+    ]
+    query = (parts[0].astype(jnp.float32) * width ** (-0.5)).astype(jnp.bfloat16)
+    return query, parts[1], parts[2]
 
 
 def softmax_of(query, key, bias):
-    scores = contract_columns(query, key) + bias
+    scores = batch_columns(query, key) + bias
     raised = jnp.exp(scores - jnp.max(scores, -1, keepdims=True))
-    return raised / jnp.sum(raised, -1, keepdims=True)
+    return raised * (1.0 / jnp.sum(raised, -1, keepdims=True))
 
 
 def attention_forward(projected, bias_grid, images, groups, width):
     rows, total = projected.shape
     tokens, wide = rows // images, total // groups
-    per_group = bias_grid.shape[0] // groups
+    count = bias_grid.shape[0] // groups
+    front = wide * 3 // 4
 
     def body(block_ref, bias_ref, out_ref):
-        out = []
-        for j, (query, key, value) in enumerate(heads_of(block_ref[...], width)):
-            weights = softmax_of(query, key, bias_ref[j]).astype(jnp.bfloat16)
-            out.append(jnp.dot(weights, value, preferred_element_type=jnp.float32))
-        out_ref[:, : wide * 3 // 4] = jnp.zeros((tokens, wide * 3 // 4), jnp.bfloat16)
-        out_ref[:, wide * 3 // 4 :] = jnp.concatenate(out, 1).astype(jnp.bfloat16)
-
-    spec = pl.BlockSpec((tokens, wide), lambda b, g: (g, b))
+        for g in range(images):
+            own = slice(g * tokens, (g + 1) * tokens)
+            query, key, value = heads_of(block_ref[own, :], count, width)
+            weights = softmax_of(query, key, bias_ref[...]).astype(jnp.bfloat16)
+            out = batch_matmul(weights, value)
+            out_ref[own, :front] = jnp.zeros((tokens, front), jnp.bfloat16)
+            out_ref[own, front:] = jnp.concatenate(list(out), 1).astype(jnp.bfloat16)
+
+    spec = pl.BlockSpec((rows, wide), lambda b: (0, b))
     return pl.pallas_call(
         body,
         out_shape=jax.ShapeDtypeStruct((rows, total), jnp.bfloat16),
-        grid=(groups, images),
-        in_specs=[spec, pl.BlockSpec((per_group, tokens, tokens), lambda b, g: (b, 0, 0))],
+        grid=(groups,),
+        in_specs=[spec, pl.BlockSpec((count, tokens, tokens), lambda b: (b, 0, 0))],
         out_specs=spec,
         compiler_params=pltpu.CompilerParams(vmem_limit_bytes=32 * 2**20),
         cost_estimate=LIGHT,
@@ -740,45 +823,46 @@
 def attention_backward(projected, grad_context, bias_grid, bias_grad, images, groups, width):
     rows, total = projected.shape
     tokens, wide = rows // images, total // groups
-    per_group = bias_grid.shape[0] // groups
-
-    def body(block_ref, grad_ref, bias_ref, before_ref, out_ref, bias_out):
-        image = pl.program_id(1)
-
-        @pl.when(image == 0)
-        def _():
-            bias_out[...] = before_ref[...]
-
-        out = []
-        grads = grad_ref[:, wide * 3 // 4 :]
-        for j, (query, key, value) in enumerate(heads_of(block_ref[...], width)):
-            weights = softmax_of(query, key, bias_ref[j])
-            grad = grads[:, j * width : (j + 1) * width]
-            grad_weights = contract_columns(grad, value)
-            grad_value = contract_first(weights.astype(jnp.bfloat16), grad)
+    count = bias_grid.shape[0] // groups
+    front = wide * 3 // 4
+
+    def body(block_ref, grad_ref, bias_ref, *rest):
+        before_ref, (out_ref, bias_out) = rest[:-2], rest[-2:]
+        bias_total = before_ref[0][...] if before_ref else 0.0
+        for g in range(images):
+            own = slice(g * tokens, (g + 1) * tokens)
+            query, key, value = heads_of(block_ref[own, :], count, width)
+            grads = grad_ref[own, front:]
+            grad = jnp.stack([grads[:, j * width : (j + 1) * width] for j in range(count)])
+            weights = softmax_of(query, key, bias_ref[...])
+            grad_weights = batch_columns(grad, value)
+            grad_value = batch_rows(weights.astype(jnp.bfloat16), grad)
             inner = jnp.sum(weights * grad_weights, -1, keepdims=True)
             grad_scores = weights * (grad_weights - inner)
-            bias_out[j] += grad_scores
+            bias_total = bias_total + grad_scores
             rounded = grad_scores.astype(jnp.bfloat16)
-            grad_query = jnp.dot(rounded, key, preferred_element_type=jnp.float32) * width ** (-0.5)
-            out += [grad_query, contract_first(rounded, query), grad_value]
-        out_ref[:, : wide * 3 // 4] = jnp.concatenate(out, 1).astype(jnp.bfloat16)
-        out_ref[:, wide * 3 // 4 :] = jnp.zeros((tokens, wide // 4), jnp.bfloat16)
-
-    spec = pl.BlockSpec((tokens, wide), lambda b, g: (g, b))
-    bias_spec = pl.BlockSpec((per_group, tokens, tokens), lambda b, g: (b, 0, 0))
+            grad_query = batch_matmul(rounded, key) * width ** (-0.5)
+            grad_key = batch_rows(rounded, query)
+            out = [part[j] for j in range(count) for part in (grad_query, grad_key, grad_value)]
+            out_ref[own, :front] = jnp.concatenate(out, 1).astype(jnp.bfloat16)
+            out_ref[own, front:] = jnp.zeros((tokens, wide - front), jnp.bfloat16)
+        bias_out[...] = bias_total
+
+    spec = pl.BlockSpec((rows, wide), lambda b: (0, b))
+    bias_spec = pl.BlockSpec((count, tokens, tokens), lambda b: (b, 0, 0))
+    operands = [projected, grad_context, bias_grid] + ([] if bias_grad is None else [bias_grad])
     return pl.pallas_call(
         body,
         out_shape=(
             jax.ShapeDtypeStruct((rows, total), jnp.bfloat16),
             jax.ShapeDtypeStruct(bias_grid.shape, jnp.float32),
         ),
-        grid=(groups, images),
-        in_specs=[spec, spec, bias_spec, bias_spec],
+        grid=(groups,),
+        in_specs=[spec, spec] + [bias_spec] * (len(operands) - 2),
         out_specs=(spec, bias_spec),
         compiler_params=pltpu.CompilerParams(vmem_limit_bytes=40 * 2**20),
         cost_estimate=LIGHT,
-    )(projected, grad_context, bias_grid, bias_grad)
+    )(*operands)
 
 
 def gelu_parts(hidden):
@@ -1008,11 +1092,10 @@
     choose = (chosen[:, None] == jnp.arange(rows)[None, :]).astype(jnp.bfloat16)
     picked = jnp.dot(choose, final_rows, preferred_element_type=jnp.float32).astype(jnp.bfloat16)
     if place.short:
-        rows_ring = place.ring(picked, "z")
-        rows_ring[2] = await_hops([(head_group, "two"), (head_group, "near")], rows_ring[2])
+        rows_ring = [picked] + [place.turn(picked, k) for k in range(1, tensor_size)]
+        rows_ring = await_hops([(head_group, "two"), (head_group, "near")], *rows_ring)
         head_group.start("far")
-        rows_ring[3:] = [place.hop(rows_ring[2], "z")]
-        rows_ring[3] = await_hops([(head_group, "far")], rows_ring[3])
+        rows_ring = await_hops([(head_group, "far")], *rows_ring)
         head_full = assemble(place, head_group, 0, head_weight.shape[0], "xyc", "")
     else:
         rows_ring = place.ring(picked, "z")
@@ -1049,8 +1132,7 @@
         turn(grad_rows_all[step].astype(jnp.bfloat16), tensor_size - step)
         for step in range(1, tensor_size)
     ]
-    if returned:
-        returned[0], grad_logits = lax.optimization_barrier((returned[0], grad_logits))
+    *returned, grad_logits = lax.optimization_barrier((*returned, grad_logits))
     grad_picked = grad_rows_all[0]
     for part in returned:
         grad_picked = grad_picked + part.astype(jnp.float32)
@@ -1080,7 +1162,7 @@
     grad_final_gain, grad_final_shift = final_sums[0], final_sums[1]
     scale_sum = final_sums[2]
 
-    bias_grad = jnp.zeros(bias_grid.shape, jnp.float32)
+    bias_grad = None
     layer_grads = [None] * layer_count
     attention_grads = [None] * layer_count
     hidden_grads = [None] * layer_count
@@ -1130,9 +1212,16 @@
             projected, grad_context, bias_grid, bias_grad, images, heads_size, head_width
         )
         grad_projected, bias_grad = step(grad_projected, bias_grad)
+        grad_normed = contract_columns(grad_projected, full)
+        output_below = saved_layers[layer_at - 1][10] if layer_at else None
+        grad_residual, sums, *grad_below = norm_backward(
+            residual_in, grad_normed, grad_middle, output_below, vector_table, base, base - 1, images
+        )
+        grad_rows[0], grad_rows[1], scale_sum = sums[0], sums[1], sums[2]
+        grad_projected, grad_residual = lax.optimization_barrier((grad_projected, grad_residual))
         pairs = [(normed, grad_projected), (grad_attended, context)]
         if place.short:
-            attention_grads[layer_at] = send([pairs], "xz", "yc")
+            packed = packed_gradient(place, pairs, "xz", "yc")
         else:
             whole = sum(contract_rows(a, b) for a, b in pairs)
             attention_grads[layer_at] = scatter_sum(
@@ -1141,50 +1230,51 @@
                 ),
                 "ycxz",
             )
-        grad_normed = contract_columns(grad_projected, full)
-        if place.short and layer_at == 0:
-            grad_normed = pump([attention_grads[0]], grad_normed)
-        output_below = saved_layers[layer_at - 1][10] if layer_at else None
-        grad_residual, sums, *grad_below = norm_backward(
-            residual_in, grad_normed, grad_middle, output_below, vector_table, base, base - 1, images
+        leaves, form = jax.tree.flatten(packed if place.short else ())
+        grad_residual, *rest = step(grad_residual, *grad_below, *leaves) if (grad_below or leaves) else (
+            grad_residual,
         )
-        grad_rows[0], grad_rows[1], scale_sum = sums[0], sums[1], sums[2]
         if layer_at:
-            grad_residual, grad_output = step(grad_residual, grad_below[0])
-        else:
-            grad_residual = step(grad_residual)
+            grad_output = rest.pop(0)
+        if place.short:
+            sent, kept = jax.tree.unflatten(form, rest)
+            attention_grads[layer_at] = Scatter(place, [sent], [kept])
+            movers.append(attention_grads[layer_at])
         layer_grads[layer_at] = jnp.stack(grad_rows)
     grad_residual = grad_residual.reshape(images, padded, wide)
     held_out = is_masked | (token_ids >= patch_count)[None, :, None]
     grad_embedded = low(jnp.where(held_out, 0.0, grad_residual)).reshape(rows, wide)
     if place.short:
-        patch_mover = send([[(local_pixels, grad_embedded)]], "xycz", "")
+        leaves, form = jax.tree.flatten(
+            packed_gradient(place, [(local_pixels, grad_embedded)], "xycz", "")
+        )
+        *leaves, bias_grad, grad_residual = step(*leaves, bias_grad, grad_residual)
+        packed = jax.tree.unflatten(form, leaves)
+        patch_mover = Brief(place, *packed)
+        movers.insert(0, patch_mover)
+        attention_grads[0].rider = patch_mover
     else:
         patch_sum = contract_rows(local_pixels, grad_embedded)
-    bias_grad, grad_residual = lax.optimization_barrier((bias_grad, grad_residual))
+    relative_grad = bias_collect(bias_rows(bias_grad, GRID), bias_corners(bias_grad, GRID), GRID)
     grad_class = jnp.sum(grad_residual[:, patch_count], 0)
     grad_mask = jnp.sum(jnp.where(is_masked, grad_residual, 0.0), (0, 1))
     vector_grad = jnp.concatenate(
         layer_grads + [jnp.stack([grad_final_gain, grad_final_shift, grad_class, grad_mask])], 0
     )
-    collected = step(bias_rows(bias_grad, GRID))
-    if place.short:
-        for mover in movers:
-            if mover.total is not None:
-                mover.total, collected = lax.optimization_barrier((mover.total, collected))
-    relative_grad = bias_collect(collected, bias_corners(bias_grad, GRID), GRID)
-
     counts = (1, vector_grad.size, relative_grad.size)
     flat = jnp.concatenate([loss_part.reshape(1), vector_grad.reshape(-1), relative_grad.reshape(-1)])
     flat = jnp.pad(flat, (0, -flat.size % 1024)).reshape(-1, 128)
     if place.short:
+        for mover in movers:
+            if mover.total is not None:
+                mover.total, flat = lax.optimization_barrier((mover.total, flat))
         flat = step(flat)
         small = SmallSum(place, flat)
         movers.append(small)
         while any(m.flying for m in movers):
             place.scalars = pump(movers, place.scalars)
         flat = small.total
-        patch_grad = patch_mover.total[0][:each]
+        patch_grad = patch_mover.total[:each]
         head_grad = head_mover.total[0]
         attention_grads = [m.total[0] for m in attention_grads]
         hidden_grads = [m.total for m in hidden_grads]

time: 688 us -> 669 us (0.972)
  Pallas kernels: 174 us -> 151 us
  waiting for transfers between devices: 202 us -> 217 us
  local copies, waits for them, and re-layouts: 88.4 us -> 79.5 us
  starting transfers between devices: 89.9 us -> 82.4 us
    ppermute x53 -> x34, waiting for transfers between devices: 148 us -> 100 us  [hop(): lax.ppermute(value, axis, [(i, (i + 1) % count) for i in range(count)])]
    ppermute x3 -> x20, waiting for transfers between devices: 0.01 us -> 46.4 us  [the longest x18 46.3 us: turn(): return lax.ppermute(value, 'tensor', pairs)]
    ppermute x57 -> x56, waiting for transfers between devices: 27.8 us -> 53 us  [hop(): return lax.ppermute(value, 'heads', pairs)]
    ppermute x53 -> x34, starting transfers between devices: 48.6 us -> 25.7 us  [hop(): lax.ppermute(value, axis, [(i, (i + 1) % count) for i in range(count)])]
    ppermute x3 -> x20, starting transfers between devices: 3.88 us -> 19.7 us  [the longest x18 16.7 us: turn(): return lax.ppermute(value, 'tensor', pairs)]
    pallas_call x18 -> x15, Pallas kernels: 33.6 us -> 23.2 us  [merged(): pl.pallas_call(body, out_shape=shapes, grid=(depth,), in_specs=blocks, ou...]
    pallas_call x2, Pallas kernels: 35 us -> 26.3 us  [attention_backward(): pl.pallas_call(body, out_shape=(jax.ShapeDtypeStruct((rows, total), jnp.b...]
    unnamed x386 -> x394, local copies, waits for them, and re-layouts: 57.9 us -> 49.8 us
  transfers between devices with their start and end apart: 119 -> 116, of which waited for: 55 -> 46; matrix products, arithmetic and copies ran while one was open for 16% -> 18% of each run, Pallas kernels for 20% -> 18%
where the time goes in v1:
time: 669 us; the launch traced here: 660 us
  waiting for transfers between devices  217 us (32%)
  Pallas kernels  151 us (23%)
  starting transfers between devices  82.4 us (12%)
  local copies, waits for them, and re-layouts  79.5 us (12%)
  matrix products  78 us (12%)
  other arithmetic  44.9 us (7%)
    ppermute x34, waiting for transfers between devices, hop(): lax.ppermute(value, axis, [(i, (i + 1) % count) for i in range(count)])  100 us
    pallas_call x8, Pallas kernels, packed_gradient(): pl.pallas_call(body, out_shape=[jax.ShapeDtypeStruct(shape, jnp.bfloat16)...  54.7 us
    ppermute x56, waiting for transfers between devices, hop(): return lax.ppermute(value, 'heads', pairs)  53 us
    unnamed x394, local copies, waits for them, and re-layouts  49.8 us
    ppermute x18, waiting for transfers between devices, turn(): return lax.ppermute(value, 'tensor', pairs)  46.3 us
    ppermute x56, starting transfers between devices, hop(): return lax.ppermute(value, 'heads', pairs)  28.9 us
    dot_general x9, matrix products, contract_columns(): lax.dot_general(left_side, right_side, (((1,), (1,)), ((), ())), preferre...  27.1 us
    pallas_call x2, Pallas kernels, attention_backward(): pl.pallas_call(body, out_shape=(jax.ShapeDtypeStruct((rows, total), jnp.b...  26.3 us
  transfers between devices with their start and end apart: 116, of which 46 were waited for; matrix products, arithmetic and copies ran while one was open for 18% of the time, Pallas kernels for 18%

profile of v1, /device:TPU:0, one launch (start us, length us, event | category | flops | bytes accessed | tf_op | source)
XLA Modules:
  0.0 660.1 jit_solution(644787974109864418)
XLA Ops:
  6.0 6.8 %collective-permute-done = bf16[1,128,768]{2,1,0:T(8,128)(2,1)S(1)} collective-permute-done((bf16[1,128,768]{2,1,0:T(8,128)(2,1)S(1)}, bf16[1,128,768]{2,1,0:T(8,128)(2,1)S(1)}, u32[]{:S(2)}, u32[]{:S(2)}) %collective-permute-start) | collective-permute-done | bytes 196640 | tf_op jit(solution)/shard_map/ppermute | solution.py:51
  12.8 7.9 %collective-permute-done.1 = bf16[1,128,768]{2,1,0:T(8,128)(2,1)S(1)} collective-permute-done((bf16[1,128,768]{2,1,0:T(8,128)(2,1)S(1)}, bf16[1,128,768]{2,1,0:T(8,128)(2,1)S(1)}, u32[]{:S(2)}, u32[]{:S(2)}) %collective-permute-start.1) | collective-permute-done | bytes 196640 | tf_op jit(solution)/shard_map/ppermute | solution.py:51
  33.5 8.6 %collective-permute-done.3 = bf16[2,96,768]{2,1,0:T(8,128)(2,1)} collective-permute-done((bf16[2,96,768]{2,1,0:T(8,128)(2,1)S(1)}, bf16[2,96,768]{2,1,0:T(8,128)(2,1)}, u32[]{:S(2)}, u32[]{:S(2)}) %collective-permute-start.3) | collective-permute-done | bytes 294944 | tf_op jit(solution)/shard_map/ppermute | solution.py:51
  42.9 8.1 %collective-permute-done.4 = bf16[2,96,768]{2,1,0:T(8,128)(2,1)} collective-permute-done((bf16[2,96,768]{2,1,0:T(8,128)(2,1)}, bf16[2,96,768]{2,1,0:T(8,128)(2,1)}, u32[]{:S(2)}, u32[]{:S(2)}) %collective-permute-start.4) | collective-permute-done | bytes 294944 | tf_op jit(solution)/shard_map/ppermute | solution.py:51
  109.9 10.1 %collective-permute-done.25 = bf16[2,96,768]{2,1,0:T(8,128)(2,1)S(1)} collective-permute-done((bf16[2,96,768]{2,1,0:T(8,128)(2,1)S(1)}, bf16[2,96,768]{2,1,0:T(8,128)(2,1)S(1)}, u32[]{:S(2)}, u32[]{:S(2)}) %collective-permute-start.25) | collective-permute-done | bytes 294944 | tf_op jit(solution)/shard_map/ppermute | solution.py:51
  173.0 11.4 %collective-permute-done.40.refs_4_ = bf16[4,2,96,768]{3,2,1,0:T(8,128)(2,1)S(1)} collective-permute-done((bf16[4,2,96,768]{3,2,1,0:T(8,128)(2,1)S(1)}, bf16[4,2,96,768]{3,2,1,0:T(8,128)(2,1)S(1)}, u32[]{:S(2)}, u32[]{:S(2)}) %collective-permute-start.40) | collective-permute-done | bytes 1179680 | tf_op jit(solution)/shard_map/ppermute | solution.py:51
  188.4 12.3 %collective-permute-done.42.refs_7_ = bf16[2,2,96,768]{3,2,1,0:T(8,128)(2,1)} collective-permute-done((bf16[2,2,96,768]{3,2,1,0:T(8,128)(2,1)S(1)}, bf16[2,2,96,768]{3,2,1,0:T(8,128)(2,1)}, u32[]{:S(2)}, u32[]{:S(2)}) %collective-permute-start.42) | collective-permute-done | bytes 589856 | tf_op jit(solution)/shard_map/ppermute | solution.py:64
  243.4 13.8 %collective-permute-done.51 = bf16[150,768]{1,0:T(8,128)(2,1)} collective-permute-done((bf16[150,768]{1,0:T(8,128)(2,1)}, bf16[150,768]{1,0:T(8,128)(2,1)}, u32[]{:S(2)}, u32[]{:S(2)}) %collective-permute-start.51) | collective-permute-done | bytes 230432 | tf_op jit(solution)/shard_map/ppermute | solution.py:69
  299.1 7.9 %collective-permute-done.64 = bf16[150,768]{1,0:T(8,128)(2,1)S(1)} collective-permute-done((bf16[150,768]{1,0:T(8,128)(2,1)S(1)}, bf16[150,768]{1,0:T(8,128)(2,1)S(1)}, u32[]{:S(2)}, u32[]{:S(2)}) %collective-permute-start.64) | collective-permute-done | bytes 230432 | tf_op jit(solution)/shard_map/ppermute | solution.py:1117
  317.2 6.8 %shard_map.413 = (bf16[2,2,4,96,768]{4,3,2,1,0:T(8,128)(2,1)}, f32[4,96,768]{2,1,0:T(8,128)S(1)}, f32[4,96,768]{2,1,0:T(8,128)S(1)}, f32[4,96,768]{2,1,0:T(8,128)S(1)}, f32[4,96,768]{2,1,0:T(8,128)S(1)}) custom-call(s32[4]{0:T(128)S(1)} %pad_add_fusion.scalars, bf16[416,768]{1,0:T(8,128)(2,1)S(1)} %get-tuple-element.483.refs_0_, bf16[416,3072]{1,0:T(8,128)(2,1)} %copy-done.153), custom_call_target="tpu_custom_call" | custom-call | flops 1 | bytes 1 | tf_op jit(solution)/shard_map/pallas_call | solution.py:480
  324.3 9.3 %fusion.5.refs_1_ = bf16[416,3072]{1,0:T(8,128)(2,1)} fusion(f32[416,3072]{1,0:T(8,128)} %get-tuple-element.768, bf16[416,768]{1,0:T(8,128)(2,1)S(1)} %get-tuple-element.483.refs_0_, bf16[768,3072]{1,0:T(8,128)(2,1)} %copy-done.47), kind=kOutput, calls=%fused_computation.9 | convolution fusion | flops 1975713792 | bytes 13025280 | tf_op jit(solution)/shard_map/dot_general | solution.py:1185
  335.1 6.8 %shard_map.412 = (bf16[2,2,4,96,768]{4,3,2,1,0:T(8,128)(2,1)}, f32[4,96,768]{2,1,0:T(8,128)S(1)}, f32[4,96,768]{2,1,0:T(8,128)S(1)}, f32[4,96,768]{2,1,0:T(8,128)S(1)}, f32[4,96,768]{2,1,0:T(8,128)S(1)}) custom-call(s32[4]{0:T(128)S(1)} %pad_add_fusion.scalars, bf16[416,768]{1,0:T(8,128)(2,1)S(1)} %copy-done.130, bf16[416,3072]{1,0:T(8,128)(2,1)} %fusion.5.refs_1_), custom_call_target="tpu_custom_call" | custom-call | flops 1 | bytes 1 | tf_op jit(solution)/shard_map/pallas_call | solution.py:480
  361.8 12.7 %shard_map.417 = (bf16[416,3072]{1,0:T(8,128)(2,1)S(1)}, f32[12,208,208]{2,1,0:T(8,128)S(1)}) custom-call(bf16[416,3072]{1,0:T(8,128)(2,1)S(1)} %copy-done.15, bf16[416,3072]{1,0:T(8,128)(2,1)S(1)} %convolution_convert_fusion.1.grad_ref, f32[12,208,208]{2,1,0:T(8,128)S(1)} %shard_map.393.bias_ref), custom_call_target="tpu_custom_call" | custom-call | flops 1 | bytes 1 | tf_op jit(solution)/shard_map/pallas_call | solution.py:854
  393.6 10.1 %shard_map.420 = (bf16[2,2,4,96,768]{4,3,2,1,0:T(8,128)(2,1)}, f32[4,96,768]{2,1,0:T(8,128)S(1)}, f32[4,96,768]{2,1,0:T(8,128)S(1)}, f32[4,96,768]{2,1,0:T(8,128)S(1)}, f32[4,96,768]{2,1,0:T(8,128)S(1)}) custom-call(s32[4]{0:T(128)S(1)} %pad_add_fusion.scalars, bf16[416,768]{1,0:T(8,128)(2,1)S(1)} %copy-done.121, bf16[416,3072]{1,0:T(8,128)(2,1)} %copy-done.61, ...), custom_call_target="tpu_custom_call" | custom-call | flops 1 | bytes 1 | tf_op jit(solution)/shard_map/pallas_call | solution.py:480
  403.7 8.9 %collective-permute-done.75.refs_4_ = bf16[2,4,96,768]{3,2,1,0:T(8,128)(2,1)} collective-permute-done((bf16[2,4,96,768]{3,2,1,0:T(8,128)(2,1)}, bf16[2,4,96,768]{3,2,1,0:T(8,128)(2,1)}, u32[]{:S(2)}, u32[]{:S(2)}) %collective-permute-start.75) | collective-permute-done | bytes 1179680 | tf_op jit(solution)/shard_map/ppermute | solution.py:51
  424.1 7.9 %fusion.11.refs_1_ = bf16[416,3072]{1,0:T(8,128)(2,1)} fusion(f32[416,3072]{1,0:T(8,128)} %get-tuple-element.766, bf16[416,768]{1,0:T(8,128)(2,1)S(1)} %copy-done.132, bf16[768,3072]{1,0:T(8,128)(2,1)} %copy-done.45), kind=kOutput, calls=%fused_computation.15 | convolution fusion | flops 1975713792 | bytes 13025280 | tf_op jit(solution)/shard_map/dot_general | solution.py:1185
  432.0 6.9 %shard_map.424 = (bf16[2,2,4,96,768]{4,3,2,1,0:T(8,128)(2,1)}, f32[4,96,768]{2,1,0:T(8,128)S(1)}, f32[4,96,768]{2,1,0:T(8,128)S(1)}, f32[4,96,768]{2,1,0:T(8,128)S(1)}, f32[4,96,768]{2,1,0:T(8,128)S(1)}) custom-call(s32[4]{0:T(128)S(1)} %pad_add_fusion.scalars, bf16[416,768]{1,0:T(8,128)(2,1)S(1)} %copy-done.133, bf16[416,3072]{1,0:T(8,128)(2,1)} %copy-done.152), custom_call_target="tpu_custom_call" | custom-call | flops 1 | bytes 1 | tf_op jit(solution)/shard_map/pallas_call | solution.py:480
  444.0 6.8 %shard_map.423 = (bf16[2,2,4,96,768]{4,3,2,1,0:T(8,128)(2,1)}, f32[4,96,768]{2,1,0:T(8,128)S(1)}, f32[4,96,768]{2,1,0:T(8,128)S(1)}, f32[4,96,768]{2,1,0:T(8,128)S(1)}, f32[4,96,768]{2,1,0:T(8,128)S(1)}) custom-call(s32[4]{0:T(128)S(1)} %pad_add_fusion.scalars, bf16[416,768]{1,0:T(8,128)(2,1)S(1)} %copy-done.127, bf16[416,3072]{1,0:T(8,128)(2,1)} %fusion.11.refs_1_), custom_call_target="tpu_custom_call" | custom-call | flops 1 | bytes 1 | tf_op jit(solution)/shard_map/pallas_call | solution.py:480
  475.6 13.6 %shard_map.428 = (bf16[416,3072]{1,0:T(8,128)(2,1)S(1)}, f32[12,208,208]{2,1,0:T(8,128)S(1)}) custom-call(bf16[416,3072]{1,0:T(8,128)(2,1)S(1)} %copy-done.11, bf16[416,3072]{1,0:T(8,128)(2,1)S(1)} %convolution_convert_fusion.grad_ref, f32[12,208,208]{2,1,0:T(8,128)S(1)} %shard_map.393.bias_ref, f32[12,208,208]{2,1,0:T(8,128)} %copy-done.59), custom_call_target="tpu_custom_call" | custom-call | flops 1 | bytes 1 | tf_op jit(solution)/shard_map/pallas_call | solution.py:854
  510.1 10.2 %shard_map.433 = (bf16[2,2,4,96,768]{4,3,2,1,0:T(8,128)(2,1)}, f32[4,96,768]{2,1,0:T(8,128)S(1)}, f32[4,96,768]{2,1,0:T(8,128)S(1)}, f32[4,96,768]{2,1,0:T(8,128)S(1)}, f32[4,96,768]{2,1,0:T(8,128)S(1)}) custom-call(s32[4]{0:T(128)S(1)} %pad_add_fusion.scalars, bf16[416,768]{1,0:T(8,128)(2,1)S(1)} %shard_map.395.refs_0_, bf16[416,3072]{1,0:T(8,128)(2,1)} %copy-done.60, ...), custom_call_target="tpu_custom_call" | custom-call | flops 1 | bytes 1 | tf_op jit(solution)/shard_map/pallas_call | solution.py:480
  520.4 9.8 %collective-permute-done.90.refs_4_ = bf16[2,4,96,768]{3,2,1,0:T(8,128)(2,1)} collective-permute-done((bf16[2,4,96,768]{3,2,1,0:T(8,128)(2,1)}, bf16[2,4,96,768]{3,2,1,0:T(8,128)(2,1)}, u32[]{:S(2)}, u32[]{:S(2)}) %collective-permute-start.90) | collective-permute-done | bytes 1179680 | tf_op jit(solution)/shard_map/ppermute | solution.py:51
  552.3 11.1 %collective-permute-done.92 = bf16[1,96,768]{2,1,0:T(8,128)(2,1)S(1)} collective-permute-done((bf16[1,96,768]{2,1,0:T(8,128)(2,1)S(1)}, bf16[1,96,768]{2,1,0:T(8,128)(2,1)S(1)}, u32[]{:S(2)}, u32[]{:S(2)}) %collective-permute-start.92) | collective-permute-done | bytes 147488 | tf_op jit(solution)/shard_map/ppermute | solution.py:69
  603.2 15.5 %collective-permute-done.101 = bf16[4,32,768]{2,1,0:T(8,128)(2,1)S(1)} collective-permute-done((bf16[4,32,768]{2,1,0:T(8,128)(2,1)S(1)}, bf16[4,32,768]{2,1,0:T(8,128)(2,1)S(1)}, u32[]{:S(2)}, u32[]{:S(2)}) %collective-permute-start.101) | collective-permute-done | bytes 196640 | tf_op jit(solution)/shard_map/ppermute | solution.py:64
  634.7 12.5 %collective-permute-done.108 = bf16[1,128,768]{2,1,0:T(8,128)(2,1)S(1)} collective-permute-done((bf16[1,128,768]{2,1,0:T(8,128)(2,1)S(1)}, bf16[1,128,768]{2,1,0:T(8,128)(2,1)S(1)}, u32[]{:S(2)}, u32[]{:S(2)}) %collective-permute-start.108) | collective-permute-done | bytes 196640 | tf_op jit(solution)/shard_map/ppermute | solution.py:69
  (810 shorter events, 417.5 us)
Async XLA Ops:
  33.5 23.8 %collective-permute-start.9 = (bf16[4,1,128,768]{3,2,1,0:T(8,128)(2,1)S(1)}, bf16[4,1,128,768]{3,2,1,0:T(8,128)(2,1)}, u32[]{:S(2)}, u32[]{:S(2)}) collective-permute-start(bf16[4,1,128,768]{3,2,1,0:T(8,128)(2,1)S(1)} %pad_maximum_fusion.5.refs_0_), channel_id=1, source_target_pairs={{0,4},{4,0},{8,12},{12,8},{1,5},{5,1},{9,13},{13,9},{2,6},{6,2},{1... | collective-permute-start | bytes 2359304 | tf_op jit(solution)/shard_map/ppermute | solution.py:64
  77.2 32.8 %collective-permute-start.22 = (bf16[4,2,96,768]{3,2,1,0:T(8,128)(2,1)S(1)}, bf16[4,2,96,768]{3,2,1,0:T(8,128)(2,1)S(1)}, u32[]{:S(2)}, u32[]{:S(2)}) collective-permute-start(bf16[4,2,96,768]{3,2,1,0:T(8,128)(2,1)S(1)} %pad_maximum_fusion.1.refs_0_), channel_id=1, source_target_pairs={{0,4},{4,0},{8,12},{12,8},{1,5},{5,1},{9,13},{13,9},{2,6},{6,2},{1... | collective-permute-start | bytes 3538952 | tf_op jit(solution)/shard_map/ppermute | solution.py:64
  77.3 28.3 %collective-permute-start.18 = (bf16[4,2,96,768]{3,2,1,0:T(8,128)(2,1)S(1)}, bf16[4,2,96,768]{3,2,1,0:T(8,128)(2,1)S(1)}, u32[]{:S(2)}, u32[]{:S(2)}) collective-permute-start(bf16[4,2,96,768]{3,2,1,0:T(8,128)(2,1)S(1)} %pad_maximum_fusion.1.refs_0_), channel_id=1, source_target_pairs={{0,16},{16,0},{1,17},{17,1},{2,18},{18,2},{3,19},{19,3},{4,20},{20... | collective-permute-start | bytes 3538952 | tf_op jit(solution)/shard_map/ppermute | solution.py:51
  80.7 27.2 %collective-permute-start.17 = (bf16[4,2,96,768]{3,2,1,0:T(8,128)(2,1)S(1)}, bf16[4,2,96,768]{3,2,1,0:T(8,128)(2,1)S(1)}, u32[]{:S(2)}, u32[]{:S(2)}) collective-permute-start(bf16[4,2,96,768]{3,2,1,0:T(8,128)(2,1)S(1)} %pad_maximum_fusion.1.refs_0_), channel_id=1, source_target_pairs={{0,8},{4,12},{8,0},{12,4},{1,9},{5,13},{9,1},{13,5},{2,10},{6,14},... | collective-permute-start | bytes 3538952 | tf_op jit(solution)/shard_map/ppermute | solution.py:64
  156.4 28.0 %collective-permute-start.40 = (bf16[4,2,96,768]{3,2,1,0:T(8,128)(2,1)S(1)}, bf16[4,2,96,768]{3,2,1,0:T(8,128)(2,1)S(1)}, u32[]{:S(2)}, u32[]{:S(2)}) collective-permute-start(bf16[4,2,96,768]{3,2,1,0:T(8,128)(2,1)S(1)} %pad_maximum_fusion.2.refs_0_), channel_id=1, source_target_pairs={{0,16},{16,0},{1,17},{17,1},{2,18},{18,2},{3,19},{19,3},{4,20},{20... | collective-permute-start | bytes 3538952 | tf_op jit(solution)/shard_map/ppermute | solution.py:51
  157.0 27.7 %collective-permute-start.39 = (bf16[4,2,96,768]{3,2,1,0:T(8,128)(2,1)S(1)}, bf16[4,2,96,768]{3,2,1,0:T(8,128)(2,1)S(1)}, u32[]{:S(2)}, u32[]{:S(2)}) collective-permute-start(bf16[4,2,96,768]{3,2,1,0:T(8,128)(2,1)S(1)} %pad_maximum_fusion.2.refs_0_), channel_id=1, source_target_pairs={{0,8},{4,12},{8,0},{12,4},{1,9},{5,13},{9,1},{13,5},{2,10},{6,14},... | collective-permute-start | bytes 3538952 | tf_op jit(solution)/shard_map/ppermute | solution.py:64
  161.5 25.8 %collective-permute-start.43 = (bf16[4,2,96,768]{3,2,1,0:T(8,128)(2,1)S(1)}, bf16[4,2,96,768]{3,2,1,0:T(8,128)(2,1)S(1)}, u32[]{:S(2)}, u32[]{:S(2)}) collective-permute-start(bf16[4,2,96,768]{3,2,1,0:T(8,128)(2,1)S(1)} %pad_maximum_fusion.2.refs_0_), channel_id=1, source_target_pairs={{0,4},{4,0},{8,12},{12,8},{1,5},{5,1},{9,13},{13,9},{2,6},{6,2},{1... | collective-permute-start | bytes 3538952 | tf_op jit(solution)/shard_map/ppermute | solution.py:64
  204.5 31.1 %collective-permute-start.55 = (bf16[1,1,96,2048]{3,2,1,0:T(8,128)(2,1)}, bf16[1,1,96,2048]{3,2,1,0:T(8,128)(2,1)}, u32[]{:S(2)}, u32[]{:S(2)}) collective-permute-start(bf16[1,1,96,2048]{3,2,1,0:T(8,128)(2,1)} %convert_bitcast_fusion.refs_0_), channel_id=1, source_target_pairs={{0,4},{4,0},{8,12},{12,8},{1,5},{5,1},{9,13},{13,9},{2,6},{6,2},{1... | collective-permute-start | bytes 1179656 | tf_op jit(solution)/shard_map/ppermute | solution.py:64
  204.5 25.7 %collective-permute-start.49 = (bf16[1,1,96,2048]{3,2,1,0:T(8,128)(2,1)}, bf16[1,1,96,2048]{3,2,1,0:T(8,128)(2,1)}, u32[]{:S(2)}, u32[]{:S(2)}) collective-permute-start(bf16[1,1,96,2048]{3,2,1,0:T(8,128)(2,1)} %convert_bitcast_fusion.refs_0_), channel_id=1, source_target_pairs={{0,16},{16,0},{1,17},{17,1},{2,18},{18,2},{3,19},{19,3},{4,20},{20... | collective-permute-start | bytes 1179656 | tf_op jit(solution)/shard_map/ppermute | solution.py:51
  205.8 24.5 %collective-permute-start.48 = (bf16[1,1,96,2048]{3,2,1,0:T(8,128)(2,1)}, bf16[1,1,96,2048]{3,2,1,0:T(8,128)(2,1)}, u32[]{:S(2)}, u32[]{:S(2)}) collective-permute-start(bf16[1,1,96,2048]{3,2,1,0:T(8,128)(2,1)} %convert_bitcast_fusion.refs_0_), channel_id=1, source_target_pairs={{0,8},{4,12},{8,0},{12,4},{1,9},{5,13},{9,1},{13,5},{2,10},{6,14},... | collective-permute-start | bytes 1179656 | tf_op jit(solution)/shard_map/ppermute | solution.py:64
  231.2 26.0 %collective-permute-start.56 = (bf16[1,1,96,2048]{3,2,1,0:T(8,128)(2,1)}, bf16[1,1,96,2048]{3,2,1,0:T(8,128)(2,1)}, u32[]{:S(2)}, u32[]{:S(2)}) collective-permute-start(bf16[1,1,96,2048]{3,2,1,0:T(8,128)(2,1)} %collective-permute-done.48.refs_2_), channel_id=1, source_target_pairs={{0,4},{4,0},{8,12},{12,8},{1,5},{5,1},{9,13},{13,9},{2,6},{6,2},{1... | collective-permute-start | bytes 1179656 | tf_op jit(solution)/shard_map/ppermute | solution.py:64
  232.2 25.0 %collective-permute-start.57 = (bf16[1,1,96,2048]{3,2,1,0:T(8,128)(2,1)}, bf16[1,1,96,2048]{3,2,1,0:T(8,128)(2,1)}, u32[]{:S(2)}, u32[]{:S(2)}) collective-permute-start(bf16[1,1,96,2048]{3,2,1,0:T(8,128)(2,1)} %collective-permute-done.49.refs_4_), channel_id=1, source_target_pairs={{0,4},{4,0},{8,12},{12,8},{1,5},{5,1},{9,13},{13,9},{2,6},{6,2},{1... | collective-permute-start | bytes 1179656 | tf_op jit(solution)/shard_map/ppermute | solution.py:64
  324.1 26.4 %collective-permute-start.70 = (bf16[2,2,4,96,768]{4,3,2,1,0:T(8,128)(2,1)}, bf16[2,2,4,96,768]{4,3,2,1,0:T(8,128)(2,1)S(1)}, u32[]{:S(2)}, u32[]{:S(2)}) collective-permute-start(bf16[2,2,4,96,768]{4,3,2,1,0:T(8,128)(2,1)} %get-tuple-element.495), channel_id=1, source_target_pairs={{0,4},{4,0},{8,12},{12,8},{1,5},{5,1},{9,13},{13,9},{2,6},{6,2},{1... | collective-permute-start | bytes 7077896 | tf_op jit(solution)/shard_map/ppermute | solution.py:64
  353.4 24.9 %collective-permute-start.73 = (bf16[2,2,96,768]{3,2,1,0:T(8,128)(2,1)}, bf16[2,2,96,768]{3,2,1,0:T(8,128)(2,1)S(1)}, u32[]{:S(2)}, u32[]{:S(2)}) collective-permute-start(bf16[2,2,96,768]{3,2,1,0:T(8,128)(2,1)} %get-tuple-element.516), channel_id=1, source_target_pairs={{0,8},{4,12},{8,0},{12,4},{1,9},{5,13},{9,1},{13,5},{2,10},{6,14},... | collective-permute-start | bytes 1769480 | tf_op jit(solution)/shard_map/ppermute | solution.py:64
  354.0 24.3 %collective-permute-start.74 = (bf16[2,2,96,768]{3,2,1,0:T(8,128)(2,1)}, bf16[2,2,96,768]{3,2,1,0:T(8,128)(2,1)S(1)}, u32[]{:S(2)}, u32[]{:S(2)}) collective-permute-start(bf16[2,2,96,768]{3,2,1,0:T(8,128)(2,1)} %get-tuple-element.517), channel_id=1, source_target_pairs={{0,16},{16,0},{1,17},{17,1},{2,18},{18,2},{3,19},{19,3},{4,20},{20... | collective-permute-start | bytes 1769480 | tf_op jit(solution)/shard_map/ppermute | solution.py:51
  386.3 26.4 %collective-permute-start.75 = (bf16[2,4,96,768]{3,2,1,0:T(8,128)(2,1)}, bf16[2,4,96,768]{3,2,1,0:T(8,128)(2,1)}, u32[]{:S(2)}, u32[]{:S(2)}) collective-permute-start(bf16[2,4,96,768]{3,2,1,0:T(8,128)(2,1)} %get-tuple-element.539), channel_id=1, source_target_pairs={{0,16},{16,0},{1,17},{17,1},{2,18},{18,2},{3,19},{19,3},{4,20},{20... | collective-permute-start | bytes 3538952 | tf_op jit(solution)/shard_map/ppermute | solution.py:51
  387.1 26.3 %collective-permute-start.76 = (bf16[2,4,96,768]{3,2,1,0:T(8,128)(2,1)}, bf16[2,4,96,768]{3,2,1,0:T(8,128)(2,1)}, u32[]{:S(2)}, u32[]{:S(2)}) collective-permute-start(bf16[2,4,96,768]{3,2,1,0:T(8,128)(2,1)} %get-tuple-element.540), channel_id=1, source_target_pairs={{0,8},{4,12},{8,0},{12,4},{1,9},{5,13},{9,1},{13,5},{2,10},{6,14},... | collective-permute-start | bytes 3538952 | tf_op jit(solution)/shard_map/ppermute | solution.py:64
  469.0 26.5 %collective-permute-start.87 = (bf16[2,2,96,768]{3,2,1,0:T(8,128)(2,1)}, bf16[2,2,96,768]{3,2,1,0:T(8,128)(2,1)}, u32[]{:S(2)}, u32[]{:S(2)}) collective-permute-start(bf16[2,2,96,768]{3,2,1,0:T(8,128)(2,1)} %get-tuple-element.590), channel_id=1, source_target_pairs={{0,8},{4,12},{8,0},{12,4},{1,9},{5,13},{9,1},{13,5},{2,10},{6,14},... | collective-permute-start | bytes 1769480 | tf_op jit(solution)/shard_map/ppermute | solution.py:64
  470.2 25.4 %collective-permute-start.88 = (bf16[2,2,96,768]{3,2,1,0:T(8,128)(2,1)}, bf16[2,2,96,768]{3,2,1,0:T(8,128)(2,1)}, u32[]{:S(2)}, u32[]{:S(2)}) collective-permute-start(bf16[2,2,96,768]{3,2,1,0:T(8,128)(2,1)} %get-tuple-element.591), channel_id=1, source_target_pairs={{0,16},{16,0},{1,17},{17,1},{2,18},{18,2},{3,19},{19,3},{4,20},{20... | collective-permute-start | bytes 1769480 | tf_op jit(solution)/shard_map/ppermute | solution.py:51
  503.7 26.5 %collective-permute-start.90 = (bf16[2,4,96,768]{3,2,1,0:T(8,128)(2,1)}, bf16[2,4,96,768]{3,2,1,0:T(8,128)(2,1)}, u32[]{:S(2)}, u32[]{:S(2)}) collective-permute-start(bf16[2,4,96,768]{3,2,1,0:T(8,128)(2,1)} %get-tuple-element.625), channel_id=1, source_target_pairs={{0,16},{16,0},{1,17},{17,1},{2,18},{18,2},{3,19},{19,3},{4,20},{20... | collective-permute-start | bytes 3538952 | tf_op jit(solution)/shard_map/ppermute | solution.py:51
  504.8 26.2 %collective-permute-start.91 = (bf16[2,4,96,768]{3,2,1,0:T(8,128)(2,1)}, bf16[2,4,96,768]{3,2,1,0:T(8,128)(2,1)}, u32[]{:S(2)}, u32[]{:S(2)}) collective-permute-start(bf16[2,4,96,768]{3,2,1,0:T(8,128)(2,1)} %get-tuple-element.626), channel_id=1, source_target_pairs={{0,8},{4,12},{8,0},{12,4},{1,9},{5,13},{9,1},{13,5},{2,10},{6,14},... | collective-permute-start | bytes 3538952 | tf_op jit(solution)/shard_map/ppermute | solution.py:64
  535.9 27.5 %collective-permute-start.94 = (bf16[2,2,4,96,768]{4,3,2,1,0:T(8,128)(2,1)}, bf16[2,2,4,96,768]{4,3,2,1,0:T(8,128)(2,1)S(1)}, u32[]{:S(2)}, u32[]{:S(2)}) collective-permute-start(bf16[2,2,4,96,768]{4,3,2,1,0:T(8,128)(2,1)} %get-tuple-element.647), channel_id=1, source_target_pairs={{0,4},{4,0},{8,12},{12,8},{1,5},{5,1},{9,13},{13,9},{2,6},{6,2},{1... | collective-permute-start | bytes 7077896 | tf_op jit(solution)/shard_map/ppermute | solution.py:64
  594.0 24.7 %collective-permute-start.103 = (bf16[2,96,768]{2,1,0:T(8,128)(2,1)S(1)}, bf16[2,96,768]{2,1,0:T(8,128)(2,1)S(1)}, u32[]{:S(2)}, u32[]{:S(2)}) collective-permute-start(bf16[2,96,768]{2,1,0:T(8,128)(2,1)S(1)} %fusion.22), channel_id=1, source_target_pairs={{0,1},{1,2},{2,3},{3,0},{4,5},{5,6},{6,7},{7,4},{8,9},{9,10},{10,1... | collective-permute-start | bytes 884744 | tf_op jit(solution)/shard_map/ppermute | solution.py:69
  594.6 24.1 %collective-permute-start.104 = (bf16[1,4,96,768]{3,2,1,0:T(8,128)(2,1)S(1)}, bf16[1,4,96,768]{3,2,1,0:T(8,128)(2,1)S(1)}, u32[]{:S(2)}, u32[]{:S(2)}) collective-permute-start(bf16[1,4,96,768]{3,2,1,0:T(8,128)(2,1)S(1)} %get-tuple-element.687), channel_id=1, source_target_pairs={{0,16},{16,0},{1,17},{17,1},{2,18},{18,2},{3,19},{19,3},{4,20},{20... | collective-permute-start | bytes 1769480 | tf_op jit(solution)/shard_map/ppermute | solution.py:51
  (287 other events, 2633.8 us)
